TPU v7x, 32 devices: a whole 2x2x4 slice. The times are simulated.
32 devices in a mesh: gz: 8 (over z, y), gx: 4 (over x, core).
Axes of the slice: x: 2, y: 2, z: 4, core: 2. Of those that a mesh axis runs over, the one named last changes fastest.
Arguments:
- offsets: float32 [4, 64, 3, 64], P('gx', 'gz'), may hold values from 0 to 1
- strength: float32 [4, 64, 64], P('gx', 'gz'), may hold values from -6 to 6
- cells: int32 [4, 64, 3, 64], P('gx', 'gz'), may hold values from 0 to 252, as said below
- counts: int32 [4, 64], P('gx', 'gz'), may hold values from 0 to 64, as said below
- kx_modes: int32 [64], replicated, may hold values from 0 to 511, as said below
- ky_modes: int32 [64], replicated, may hold values from 0 to 511, as said below
Outputs:
- stream: float32 [256, 64, 128], P('gz', 'gx')
Inputs may be any that keep to these rules, and one draw needn't show every extreme that they name: `cells`: component 0 lies in 0 to 31, components 1 and 2 in 0 to 252. `counts`: some slot of some device is full in every draw. `kx_modes`: distinct indices. `ky_modes`: distinct indices.
All inputs are finite; a program needn't handle non-finite values.
Results may differ from a plain program's by a relative error of at most 0.0034.
Values sent between devices are 32-bit elements; how exact they have to be, the bound alone decides.
No kernel may reach another device: no remote copies, remote signals or barrier semaphores. Data moves between devices by JAX's collectives and lax.ppermute only.
A program may use at most 128 MiB of HBM per device.

v0:
```python
import math

import jax
import jax.numpy as jnp
from jax import lax
from jax.sharding import PartitionSpec as P

NXD = 512
KX = 64
KY = 64
ZDEV = 32
CAP = 64


def shifted(array, axis, by):
    length = lax.axis_size(axis)
    pairs = [(i, i + by) for i in range(length) if 0 <= i + by < length]
    return lax.ppermute(array, axis, pairs)


def near_part(dist):
    return 1.0 - 2.5 * dist * dist + 1.5 * dist * dist * dist


def far_part(dist):
    return 0.5 * (2.0 - dist) * (2.0 - dist) * (1.0 - dist)


def kernel_weights(frac):
    return (far_part(1.0 + frac), near_part(frac), near_part(1.0 - frac), far_part(2.0 - frac))


def spread_rows(weights, base, columns_count):
    columns = lax.broadcasted_iota(jnp.int32, (base.shape[0], columns_count), 1)
    total = jnp.zeros((base.shape[0], columns_count), jnp.float32)
    for node in range(4):
        total = total + jnp.where(columns == (base + node)[:, None], weights[node][:, None], 0.0)
    return total


def spectra(planes, kx_list, ky_list, length):
    cells_along = planes.shape[1]
    position = jnp.arange(cells_along, dtype=jnp.int32)
    phase_x = (kx_list[:, None] * position[None, :] % length).astype(jnp.float32) * (
        2.0 * jnp.pi / length
    )
    phase_y = (ky_list[:, None] * position[None, :] % length).astype(jnp.float32) * (
        2.0 * jnp.pi / length
    )
    cos_x, sin_x = (jnp.cos(phase_x), jnp.sin(phase_x))
    cos_y, sin_y = (jnp.cos(phase_y), jnp.sin(phase_y))
    high = lax.Precision.HIGHEST
    real_b = jnp.einsum("kx,zxy->zky", cos_x, planes, precision=high)
    imag_b = -jnp.einsum("kx,zxy->zky", sin_x, planes, precision=high)
    real_f = jnp.einsum("zky,qy->zkq", real_b, cos_y, precision=high) + jnp.einsum(
        "zky,qy->zkq", imag_b, sin_y, precision=high
    )
    imag_f = jnp.einsum("zky,qy->zkq", imag_b, cos_y, precision=high) - jnp.einsum(
        "zky,qy->zkq", real_b, sin_y, precision=high
    )
    return jnp.concatenate([real_f, imag_f], axis=2) * (1.0 / cells_along)


def green_terms(kx_list, ky_list, length, sigma):
    half = length // 2
    signed_x = jnp.where(kx_list >= half, kx_list - length, kx_list).astype(jnp.float32)
    signed_y = jnp.where(ky_list >= half, ky_list - length, ky_list).astype(jnp.float32)
    step = 2.0 * jnp.pi / length
    kappa = jnp.sqrt(
        sigma * sigma + step * step * (signed_x[:, None] ** 2 + signed_y[None, :] ** 2)
    )
    return (kappa, sigma / kappa)


def correlate_terms(targets, sources, kappa, amplitude, spec_four):
    distance = jnp.abs(targets[:, None] - sources[None, :]).astype(jnp.float32)
    green = amplitude[None, None] * jnp.exp(-kappa[None, None] * distance[:, :, None, None])
    result = jnp.einsum("abky,bkcy->akcy", green, spec_four, precision=lax.Precision.HIGHEST)
    return result.reshape(targets.shape[0], spec_four.shape[1], -1)


def shards(offsets, strength, cells, counts, kx_modes, ky_modes):
    offsets, strength, cells, counts = (
        lax.all_to_all(offsets, "gz", split_axis=1, concat_axis=1, tiled=True),
        lax.all_to_all(strength, "gz", split_axis=1, concat_axis=1, tiled=True),
        lax.all_to_all(cells, "gz", split_axis=1, concat_axis=1, tiled=True),
        lax.all_to_all(counts, "gz", split_axis=1, concat_axis=1, tiled=True),
    )
    slabs = lax.axis_size("gz")
    x_groups = lax.axis_size("gx")
    cells_along = NXD // 2
    padded = ZDEV + 3
    live = jnp.arange(CAP, dtype=jnp.int32)[None, :] < counts[0][:, None]
    weight_s = jnp.where(live, strength[0], 0.0).reshape(-1)
    frac_z = offsets[0, :, 0].reshape(-1)
    frac_x = offsets[0, :, 1].reshape(-1)
    frac_y = offsets[0, :, 2].reshape(-1)
    base_z = cells[0, :, 0].reshape(-1)
    base_x = cells[0, :, 1].reshape(-1)
    base_y = cells[0, :, 2].reshape(-1)
    rows_total = weight_s.shape[0]
    block = math.gcd(rows_total, 512)
    blocks = rows_total // block
    left_z = weight_s[:, None] * spread_rows(kernel_weights(frac_z), base_z, padded)
    left_x = spread_rows(kernel_weights(frac_x), base_x, cells_along)
    right_y = spread_rows(kernel_weights(frac_y), base_y, cells_along).astype(jnp.bfloat16)

    def add_block(total, pieces):
        piece_z, piece_x, piece_y = pieces
        left = (piece_z[:, :, None] * piece_x[:, None, :]).astype(jnp.bfloat16).reshape(block, -1)
        product = lax.dot_general(
            left, piece_y, (((0,), (0,)), ((), ())), preferred_element_type=jnp.float32
        )
        return (total + product, None)

    start_grid = jnp.zeros((padded * cells_along, cells_along), jnp.float32)
    grid_flat, _ = lax.scan(
        add_block,
        start_grid,
        (
            left_z.reshape(blocks, block, padded),
            left_x.reshape(blocks, block, cells_along),
            right_y.reshape(blocks, block, cells_along),
        ),
    )
    grid = grid_flat.reshape(padded, cells_along, cells_along)
    arrived = shifted(grid[ZDEV:], "gz", 1)
    own_planes = grid[:ZDEV].at[:3].add(arrived)
    spectrum = spectra(own_planes, kx_modes, ky_modes, NXD)
    summed = lax.psum_scatter(spectrum, "gx", scatter_dimension=1, tiled=True)
    kx_local = KX // x_groups
    own_kx = lax.dynamic_slice_in_dim(kx_modes, lax.axis_index("gx") * kx_local, kx_local)
    sigma = 4.0 / (ZDEV * slabs)
    kappa, amplitude = green_terms(own_kx, ky_modes, NXD, sigma)
    my_slab = lax.axis_index("gz")
    first_plane = my_slab * ZDEV
    own_index = first_plane + jnp.arange(ZDEV, dtype=jnp.int32)
    piece = lax.all_gather(summed, "gz", axis=0, tiled=True)
    count = piece.shape[0]
    source_index = jnp.arange(count, dtype=jnp.int32)
    return correlate_terms(
        own_index, source_index, kappa, amplitude, piece.reshape(count, kx_local, 2, KY)
    )


def solution(mesh):
    placed = (
        P("gx", "gz", None, None),
        P("gx", "gz", None),
        P("gx", "gz", None, None),
        P("gx", "gz"),
        P(),
        P(),
    )
    return jax.shard_map(
        shards, mesh=mesh, in_specs=placed, out_specs=P("gz", "gx", None), check_vma=False
    )
```

profile of v0, /device:TPU:0, one launch (start us, length us, event | category | flops | bytes accessed | tf_op | source)
XLA Modules:
  0.0 219.5 jit_solution(15094096626857891630)
XLA Ops:
  6.5 1.3 copy.18
  7.8 7.3 %all-to-all-start = ((s32[1,8,1]{2,0,1:T(1,128)}), s32[1,8,1]{2,0,1:T(1,128)S(1)}, u32[]{:S(2)}, u32[]{:S(2)}) async-start(s32[1,8,1]{2,0,1:T(1,128)} %copy.18), calls=%async_computation | async-start | bytes 8192 | tf_op jit(solution)/shard_map/all_to_all | solution.py:87
  15.1 0.7 copy.32
  15.8 0.7 reshape.437
  16.5 0.7 copy.33
  17.2 0.7 reshape.439
  17.9 3.7 %all-to-all-done = s32[1,8,1]{2,0,1:T(1,128)S(1)} async-done(((s32[1,8,1]{2,0,1:T(1,128)}), s32[1,8,1]{2,0,1:T(1,128)S(1)}, u32[]{:S(2)}, u32[]{:S(2)}) %all-to-all-start) | async-done | bytes 64 | tf_op jit(solution)/shard_map/all_to_all | solution.py:87
  21.6 3.3 %all-to-all-start.1 = ((f32[1,8,64]{2,0,1:T(1,128)}), f32[1,8,64]{2,0,1:T(1,128)S(1)}, u32[]{:S(2)}, u32[]{:S(2)}) async-start(f32[1,8,64]{2,0,1:T(1,128)} %bitcast.62), calls=%async_computation.1 | async-start | bytes 8192 | tf_op jit(solution)/shard_map/all_to_all | solution.py:85
  25.3 5.9 %all-to-all-done.1 = f32[1,8,64]{2,0,1:T(1,128)S(1)} async-done(((f32[1,8,64]{2,0,1:T(1,128)}), f32[1,8,64]{2,0,1:T(1,128)S(1)}, u32[]{:S(2)}, u32[]{:S(2)}) %all-to-all-start.1) | async-done | bytes 2080 | tf_op jit(solution)/shard_map/all_to_all | solution.py:85
  31.2 3.3 %all-to-all-start.3 = ((f32[8,1,192]{2,1,0:T(1,128)}), f32[8,1,192]{2,1,0:T(1,128)S(1)}, u32[]{:S(2)}, u32[]{:S(2)}) async-start(f32[8,1,192]{2,1,0:T(1,128)} %reshape.437), calls=%async_computation.3 | async-start | bytes 16384 | tf_op jit(solution)/shard_map/all_to_all | solution.py:84
  35.7 5.3 %all-to-all-done.3 = f32[8,1,192]{2,1,0:T(1,128)S(1)} async-done(((f32[8,1,192]{2,1,0:T(1,128)}), f32[8,1,192]{2,1,0:T(1,128)S(1)}, u32[]{:S(2)}, u32[]{:S(2)}) %all-to-all-start.3) | async-done | bytes 6176 | tf_op jit(solution)/shard_map/all_to_all | solution.py:84
  41.0 3.3 %all-to-all-start.2 = ((s32[8,1,192]{2,1,0:T(1,128)}), s32[8,1,192]{2,1,0:T(1,128)S(1)}, u32[]{:S(2)}, u32[]{:S(2)}) async-start(s32[8,1,192]{2,1,0:T(1,128)} %reshape.439), calls=%async_computation.2 | async-start | bytes 16384 | tf_op jit(solution)/shard_map/all_to_all | solution.py:86
  44.9 0.7 reduce.31
  46.0 4.8 %all-to-all-done.2 = s32[8,1,192]{2,1,0:T(1,128)S(1)} async-done(((s32[8,1,192]{2,1,0:T(1,128)}), s32[8,1,192]{2,1,0:T(1,128)S(1)}, u32[]{:S(2)}, u32[]{:S(2)}) %all-to-all-start.2) | async-done | bytes 6176 | tf_op jit(solution)/shard_map/all_to_all | solution.py:86
  52.6 6.4 %multiply_convert_fusion = bf16[512,35,256]{0,2,1:T(8,128)(2,1)} fusion(f32[512,256]{0,1:T(8,128)S(1)} %select_add_fusion, f32[512,35]{0,1:T(8,128)S(1)} %add_multiply_fusion), kind=kLoop, calls=%fused_computation.4 | loop fusion | flops 9175040 | bytes 9771008 | tf_op jit(solution)/shard_map/while/body/eval_jaxpr/convert_element_type | solution.py:110
  59.0 6.3 %fusion.29 = f32[8960,256]{1,0:T(8,128)S(1)} fusion(bf16[512,8960]{0,1:T(8,128)(2,1)} %bitcast.54, f32[512]{0:T(512)S(1)} %get-tuple-element.43, s32[512]{0:T(512)S(1)} %get-tuple-element.45, f32[512]{0:T(512)S(1)} %get-tuple-element.41, s32[512]{0:T(512)S(1)} %get-tuple-element.46, f32[512]{0:T(512)S(1)} %get-tuple-element.42, ...), kind=kOutput, calls=%fused_computation.34 | convolution fusion | flops 2350383104 | bytes 18366464 | tf_op jit(solution)/shard_map/while/body/eval_jaxpr/dot_general | solution.py:111
  65.5 2.7 %collective-permute-start = (f32[3,256,256]{2,1,0:T(8,128)S(1)}, f32[3,256,256]{2,1,0:T(8,128)S(1)}, u32[]{:S(2)}, u32[]{:S(2)}) collective-permute-start(f32[3,256,256]{2,1,0:T(8,128)S(1)} %bitcast.57), channel_id=1, source_target_pairs={{0,4},{4,8},{8,12},{12,16},{16,20},{20,24},{24,28},{1,5},{5,9},{9,... | collective-permute-start | bytes 2359304 | tf_op jit(solution)/shard_map/ppermute | solution.py:18
  68.7 11.1 %collective-permute-done = f32[3,256,256]{2,1,0:T(8,128)S(1)} collective-permute-done((f32[3,256,256]{2,1,0:T(8,128)S(1)}, f32[3,256,256]{2,1,0:T(8,128)S(1)}, u32[]{:S(2)}, u32[]{:S(2)}) %collective-permute-start) | collective-permute-done | bytes 786464 | tf_op jit(solution)/shard_map/ppermute | solution.py:18
  80.0 5.9 %fusion.47 = f32[32,256,64]{1,2,0:T(8,128)S(1)} fusion(f32[32,256,256]{2,1,0:T(8,128)S(1)} %add_dynamic-update-slice_fusion, s32[64]{0:T(128)S(1)} %copy-done.1), kind=kOutput, calls=%fused_computation.63 | convolution fusion | flops 1610842112 | bytes 10486016 | tf_op jit(solution)/shard_map/kx,zxy->zky/dot_general | solution.py:54
  85.9 5.9 %fusion.51 = f32[32,256,64]{1,2,0:T(8,128)S(1)} fusion(f32[32,256,256]{2,1,0:T(8,128)S(1)} %add_dynamic-update-slice_fusion, s32[64]{0:T(128)S(1)} %copy-done.1), kind=kOutput, calls=%fused_computation.67 | convolution fusion | flops 1610842112 | bytes 10486016 | tf_op jit(solution)/shard_map/kx,zxy->zky/dot_general | solution.py:53
  91.8 2.3 %fusion.7 = f32[32,64,64]{2,1,0:T(8,128)S(1)} fusion(f32[32,256,64]{1,2,0:T(8,128)S(1)} %fusion.47, s32[64]{0:T(128)S(1)} %copy-done), kind=kOutput, calls=%fused_computation.8 | convolution fusion | flops 403406848 | bytes 2621696 | tf_op jit(solution)/shard_map/zky,qy->zkq/dot_general | solution.py:58
  94.1 2.1 fusion.9
  96.2 2.1 fusion.18
  98.4 2.1 fusion.21
  100.5 1.3 maximum_multiply_fusion
  102.1 24.8 %reduce-scatter.2.cloned.1.call-done = f32[32,16,128]{2,1,0:T(8,128)} async-done(((f32[32,64,128]{2,1,0:T(8,128)}), f32[32,16,128]{2,1,0:T(8,128)}) %reduce-scatter.2.cloned.1.call-update) | async-done | bytes 262160 | tf_op jit(solution)/shard_map/reduce_scatter | solution.py:130
  127.2 11.6 %fusion.123 = f32[32,256,16,64]{1,0,3,2:T(8,128)} fusion(f32[32,256]{1,0:T(8,128)S(1)} %abs_convert_fusion, f32[16,64]{1,0:T(8,128)S(1)} %get-tuple-element.62, f32[16,64]{1,0:T(8,128)S(1)} %get-tuple-element.61), kind=kLoop, calls=%fused_computation.1.clone.clone.clone.1 | loop fusion | flops 16777216 | bytes 33595392 | tf_op jit(solution)/shard_map/abky,bkcy->akcy/dot_general | solution.py:78
  138.8 39.8 %all-gather.2.cloned.1.call-done = f32[256,16,128]{2,1,0:T(8,128)} async-done(((f32[32,16,128]{2,1,0:T(8,128)}), f32[256,16,128]{2,1,0:T(8,128)}) %all-gather.2.cloned.1.call-update) | async-done | bytes 2097168 | tf_op jit(solution)/shard_map/all_gather | solution.py:138
  178.6 1.9 copy.22
  180.5 30.3 %fusion.24 = f32[32,16,2,64]{0,2,3,1:T(2,128)S(1)} fusion(f32[256,16,2,64]{0,3,2,1:T(8,128)S(1)} %bitcast.55, f32[32,256,16,64]{1,0,3,2:T(8,128)} %fusion.123), kind=kOutput, calls=%fused_computation.21 | convolution fusion | flops 201326592 | bytes 35913728 | tf_op jit(solution)/shard_map/abky,bkcy->akcy/dot_general | solution.py:78
  210.9 0.8 copy.24
  211.6 1.0 reshape.390
  (44 shorter events, 5.6 us)
Async XLA Ops:
  7.8 13.7 %all-to-all-start = ((s32[1,8,1]{2,0,1:T(1,128)}), s32[1,8,1]{2,0,1:T(1,128)S(1)}, u32[]{:S(2)}, u32[]{:S(2)}) async-start(s32[1,8,1]{2,0,1:T(1,128)} %copy.18), calls=%async_computation | async-start | bytes 8192 | tf_op jit(solution)/shard_map/all_to_all | solution.py:87
  21.6 9.6 %all-to-all-start.1 = ((f32[1,8,64]{2,0,1:T(1,128)}), f32[1,8,64]{2,0,1:T(1,128)S(1)}, u32[]{:S(2)}, u32[]{:S(2)}) async-start(f32[1,8,64]{2,0,1:T(1,128)} %bitcast.62), calls=%async_computation.1 | async-start | bytes 8192 | tf_op jit(solution)/shard_map/all_to_all | solution.py:85
  31.2 9.8 %all-to-all-start.3 = ((f32[8,1,192]{2,1,0:T(1,128)}), f32[8,1,192]{2,1,0:T(1,128)S(1)}, u32[]{:S(2)}, u32[]{:S(2)}) async-start(f32[8,1,192]{2,1,0:T(1,128)} %reshape.437), calls=%async_computation.3 | async-start | bytes 16384 | tf_op jit(solution)/shard_map/all_to_all | solution.py:84
  41.0 9.8 %all-to-all-start.2 = ((s32[8,1,192]{2,1,0:T(1,128)}), s32[8,1,192]{2,1,0:T(1,128)S(1)}, u32[]{:S(2)}, u32[]{:S(2)}) async-start(s32[8,1,192]{2,1,0:T(1,128)} %reshape.439), calls=%async_computation.2 | async-start | bytes 16384 | tf_op jit(solution)/shard_map/all_to_all | solution.py:86
  44.4 82.6 %reduce-scatter.2.cloned.1.call-start = ((), (), s32[]{:S(2)}) async-start(), calls=%async_computation.5 | async-start | bytes 1310720 | tf_op jit(solution)/shard_map/reduce_scatter | solution.py:130
  65.5 14.5 %copy-start.1 = (s32[64]{0:T(128)S(1)}, s32[64]{0:T(128)}, u32[]{:S(2)}) copy-start(s32[64]{0:T(128)} %param.12) | copy-start | bytes 772
  65.5 14.4 %collective-permute-start = (f32[3,256,256]{2,1,0:T(8,128)S(1)}, f32[3,256,256]{2,1,0:T(8,128)S(1)}, u32[]{:S(2)}, u32[]{:S(2)}) collective-permute-start(f32[3,256,256]{2,1,0:T(8,128)S(1)} %bitcast.57), channel_id=1, source_target_pairs={{0,4},{4,8},{8,12},{12,16},{16,20},{20,24},{24,28},{1,5},{5,9},{9,... | collective-permute-start | bytes 2359304 | tf_op jit(solution)/shard_map/ppermute | solution.py:18
  80.0 11.8 %copy-start = (s32[64]{0:T(128)S(1)}, s32[64]{0:T(128)}, u32[]{:S(2)}) copy-start(s32[64]{0:T(128)} %param.13) | copy-start | bytes 772
  101.8 76.8 %all-gather.2.cloned.1.call-start = ((), (), s32[]{:S(2)}) async-start(), calls=%async_computation.6 | async-start | bytes 2359296 | tf_op jit(solution)/shard_map/all_gather | solution.py:138
Sparse Core Ops, SparseCore 0:
  102.0 24.9 reduce-scatter.1
  129.3 49.2 all-gather.1
where the time goes:
time: 220 us; the launch traced here: 219 us
  waiting for transfers between devices  95.5 us (43%)
  matrix products  57.1 us (26%)
  other arithmetic  22.2 us (10%)
  starting transfers between devices  20.3 us (9%)
  between operations  13.6 us (6%)
  local copies, waits for them, and re-layouts  10.8 us (5%)
    all_gather x1, waiting for transfers between devices, shards(): piece = lax.all_gather(summed, 'gz', axis=0, tiled=True)  39.8 us
    dot_general x1, matrix products, correlate_terms(): jnp.einsum('abky,bkcy->akcy', green, spec_four, precision=lax.Precision.H...  30.3 us
    reduce_scatter x1, waiting for transfers between devices, shards(): summed = lax.psum_scatter(spectrum, 'gx', scatter_dimension=1, tiled=True)  24.8 us
    dot_general x1, other arithmetic, correlate_terms(): jnp.einsum('abky,bkcy->akcy', green, spec_four, precision=lax.Precision.H...  11.6 us
    ppermute x1, waiting for transfers between devices, shifted(): return lax.ppermute(array, axis, pairs)  11.1 us
    all_to_all x1, starting transfers between devices, shards(): lax.all_to_all(counts, 'gz', split_axis=1, concat_axis=1, tiled=True)  7.28 us
    convert_element_type x1, other arithmetic, add_block(): (piece_z[:, :, None] * piece_x[:, None, :]).astype(jnp.bfloat16)  6.4 us
    dot_general x1, matrix products, add_block(): lax.dot_general(left, piece_y, (((0,), (0,)), ((), ())), preferred_elemen...  6.33 us
  transfers between devices with their start and end apart: 7, of which 7 were waited for; matrix products, arithmetic and copies ran while one was open for 8% of the time, Pallas kernels for 0%

commit v1 on v0

v1 whole, which is shorter than its diff:
```python
import functools
import math

import jax
import jax.numpy as jnp
from jax import lax
from jax.experimental import pallas as pl
from jax.experimental.pallas import tpu as pltpu
from jax.sharding import PartitionSpec as P

NXD = 512
ZDEV = 32
SPILL = 3
PLANES = ZDEV + SPILL

SIN_HALF = (3.14158202, -5.16714279, 2.54189899, -0.55463611)
COS_HALF = (0.99999995, -4.93479286, 4.05841191, -1.33188015, 0.21969677)


def poly(u, coefs):
    total = jnp.full_like(u, coefs[-1])
    for c in coefs[-2::-1]:
        total = total * u + c
    return total


def cos_sin_turns(turns):
    r = turns - jnp.round(turns)
    u = r * r
    s = r * poly(u, SIN_HALF)
    c2 = poly(u, tuple(2.0 * c for c in COS_HALF))
    return 1.0 - 2.0 * s * s, s * c2


def node_weights(f):
    g = 1.0 - f
    fg = -0.5 * f * g
    return (
        fg * g,
        1.0 + f * f * (1.5 * f - 2.5),
        1.0 + g * g * (1.5 * g - 2.5),
        fg * f,
    )


def node_phasors(freq):
    c1, s1 = cos_sin_turns(freq)
    c2, s2 = c1 * c1 - s1 * s1, 2.0 * c1 * s1
    return ((c1, s1), (c2, s2), (c1 * c2 - s1 * s2, s1 * c2 + c1 * s2))


def transform(freq, nodes, base, weights):
    c, s = cos_sin_turns(freq * base)
    (c1, s1), (c2, s2), (c3, s3) = nodes
    w0, w1, w2, w3 = weights
    re = w0 + w1 * c1 + w2 * c2 + w3 * c3
    im = w1 * s1 + w2 * s2 + w3 * s3
    return c * re - s * im, s * re + c * im


def spectrum_kernel(group, slab_ref, rows_ref, kx_ref, ky_ref, kappa_ref, near_ref, send_ref, acc_ref):
    kx_count = kx_ref.shape[0]
    ky_count = ky_ref.shape[0]
    blocks = rows_ref.shape[0] // 8
    kx, ky = kx_ref[...], ky_ref[...]
    kx_nodes, ky_nodes = node_phasors(kx), node_phasors(ky)
    low_lanes = lax.broadcasted_iota(jnp.int32, (4, 128), 1) < 64
    plane = lax.broadcasted_iota(jnp.int32, (40, 128), 0).astype(jnp.float32)

    def one_block(block):
        rows = rows_ref[pl.ds(pl.multiple_of(block * 8, 8), 8), :]
        turned = pltpu.roll(rows, 64, axis=1)
        left = jnp.where(low_lanes, rows[0:4], turned[4:8])
        right = jnp.where(low_lanes, turned[0:4], rows[4:8])
        w_left = node_weights(left)
        w_right = node_weights(right)
        strength = right[1:2]
        base_z, base_y = left[2:3], left[3:4]
        base_x = right[2:3]
        wz = [w[0:1] * strength for w in w_left]
        wy = [w[1:2].astype(jnp.bfloat16).astype(jnp.float32) for w in w_left]
        wx = [w[0:1] for w in w_right]
        dist = plane - base_z
        spread = jnp.where(
            dist == 0.0,
            wz[0],
            jnp.where(dist == 1.0, wz[1], jnp.where(dist == 2.0, wz[2], jnp.where(dist == 3.0, wz[3], 0.0))),
        )
        cx, sx = transform(kx, kx_nodes, base_x, wx)
        cy, sy = transform(ky, ky_nodes, base_y, wy)
        x_both = jnp.concatenate([cx, sx], axis=1)
        spread_both = jnp.concatenate([spread, spread], axis=1)
        lhs = jnp.concatenate(
            [(spread_both[z : z + 1] * x_both).astype(jnp.bfloat16) for z in range(PLANES)], axis=0
        )
        exact = jnp.concatenate(
            [jnp.concatenate([cy, -sy], axis=1), jnp.concatenate([-sy, -cy], axis=1)], axis=0
        )
        high = exact.astype(jnp.bfloat16)
        low = (exact - high.astype(jnp.float32)).astype(jnp.bfloat16)
        return lhs, jnp.concatenate([high, low], axis=0)

    def step(index, _):
        pieces = [one_block(index * group + j) for j in range(group)]
        lhs = jnp.concatenate([p[0] for p in pieces], axis=1)
        rhs = jnp.concatenate([p[1] for p in pieces], axis=1)
        product = lax.dot_general(lhs, rhs, (((1,), (1,)), ((), ())), preferred_element_type=jnp.float32)

        @pl.when(index == 0)
        def _():
            acc_ref[...] = product

        @pl.when(index > 0)
        def _():
            acc_ref[...] += product

        return 0

    lax.fori_loop(0, blocks // group, step, 0)

    slab = slab_ref[0]
    slabs = send_ref.shape[0]
    decay = jnp.exp(-kappa_ref[...])
    width = 2 * ky_count

    def plane_of(z):
        both = acc_ref[z * kx_count : (z + 1) * kx_count, :]
        return both[:, :width] + both[:, width:]

    inside = jnp.where(slab < slabs - 1, 1.0, 0.0)
    spilled = [plane_of(ZDEV + j) * inside for j in range(SPILL)]
    down = spilled[2]
    down = spilled[1] + decay * down
    down = spilled[0] + decay * down
    for z in range(ZDEV - 1, -1, -1):
        down = decay * down
        near_ref[z] = down
        down = plane_of(z) + down
    up = jnp.zeros_like(decay)
    for z in range(ZDEV):
        up = plane_of(z) + decay * up
        near_ref[z] += up
    up_near = spilled[0] + decay * up
    up_far = spilled[2] + decay * (spilled[1] + decay * up_near)
    for target in range(slabs):
        send_ref[target, 0] = jnp.where(
            target < slab, down, jnp.where(target == slab + 1, up_near, up_far)
        )
        send_ref[target, 1] = spilled[1]
        send_ref[target, 2] = spilled[2]


def far_kernel(slab_ref, near_ref, received_ref, kappa_ref, out_ref, powers_ref):
    slab = slab_ref[0]
    slabs = received_ref.shape[0]
    kappa = kappa_ref[...]
    decay = jnp.exp(-kappa)
    sigma = 4.0 / (ZDEV * slabs)
    scale = (sigma * 2.0 / NXD) / kappa
    low = jnp.zeros_like(kappa)
    high = jnp.zeros_like(kappa)
    first = jnp.zeros_like(kappa)
    second = jnp.zeros_like(kappa)
    for source in range(slabs):
        gap = slab - source
        reach = jnp.where(
            gap > 1,
            ZDEV * gap - (PLANES - 1),
            jnp.where(gap < 0, ZDEV * (-gap - 1), 0),
        ).astype(jnp.float32)
        moment = jnp.exp(-kappa * reach) * received_ref[source, 0]
        low = low + jnp.where(gap > 0, moment, 0.0)
        high = high + jnp.where(gap < 0, moment, 0.0)
        first = first + jnp.where(gap == 1, received_ref[source, 1], 0.0)
        second = second + jnp.where(gap == 1, received_ref[source, 2], 0.0)
    high = high * scale
    low = low * scale
    first = first * scale
    second = second * scale
    for z in range(ZDEV - 1, -1, -1):
        high = decay * high
        powers_ref[z] = high
    extra = {0: decay * (first + decay * second), 1: decay * second}
    source_at = {1: first, 2: second}
    for z in range(ZDEV):
        if z:
            low = decay * low
        if z in source_at:
            low = low + source_at[z]
        total = scale * near_ref[z] + low + powers_ref[z]
        if z in extra:
            total = total + extra[z]
        out_ref[z] = total


def shards(offsets, strength, cells, counts, kx_modes, ky_modes):
    slabs = lax.axis_size("gz")
    x_groups = lax.axis_size("gx")
    cap = strength.shape[-1]
    slab = lax.axis_index("gz").astype(jnp.int32).reshape(1)

    live = jnp.arange(cap, dtype=jnp.int32)[None, :] < counts[0][:, None]
    power = jnp.where(live, strength[0], 0.0)
    place = cells[0].astype(jnp.float32)
    frac = offsets[0]
    rows = jnp.stack(
        [
            jnp.concatenate([frac[:, 0], frac[:, 1]], axis=1),
            jnp.concatenate([frac[:, 2], power], axis=1),
            jnp.concatenate([place[:, 0], place[:, 1]], axis=1),
            jnp.concatenate([place[:, 2], jnp.zeros_like(power)], axis=1),
        ],
        axis=1,
    )
    sent = jnp.broadcast_to(rows[:, None], (slabs, x_groups, 4, 128)).reshape(slabs * x_groups, 4, 128)
    arrived = lax.all_to_all(sent, ("gz", "gx"), split_axis=0, concat_axis=0, tiled=True)
    arrived = arrived.reshape(-1, 128)

    kx_local = kx_modes.shape[0] // x_groups
    ky_count = ky_modes.shape[0]
    own_kx = lax.dynamic_slice_in_dim(kx_modes, lax.axis_index("gx") * kx_local, kx_local)
    kx_turns = jnp.broadcast_to((own_kx.astype(jnp.float32) / NXD)[:, None], (kx_local, 128))
    ky_turns = jnp.broadcast_to((ky_modes.astype(jnp.float32) / NXD)[:, None], (ky_count, 128))
    signed_x = jnp.where(own_kx >= NXD // 2, own_kx - NXD, own_kx).astype(jnp.float32)
    signed_y = jnp.where(ky_modes >= NXD // 2, ky_modes - NXD, ky_modes).astype(jnp.float32)
    signed_y = jnp.concatenate([signed_y, signed_y])
    sigma = 4.0 / (ZDEV * slabs)
    step = 2.0 * math.pi / NXD
    kappa = jnp.sqrt(sigma * sigma + step * step * (signed_x[:, None] ** 2 + signed_y[None, :] ** 2))

    width = 2 * ky_count
    blocks = arrived.shape[0] // 8
    group = math.gcd(blocks, 2)
    smem = pl.BlockSpec(memory_space=pltpu.SMEM)
    vmem = pl.BlockSpec(memory_space=pltpu.VMEM)
    near, moments = pl.pallas_call(
        functools.partial(spectrum_kernel, group),
        out_shape=(
            jax.ShapeDtypeStruct((ZDEV, kx_local, width), jnp.float32),
            jax.ShapeDtypeStruct((slabs, SPILL, kx_local, width), jnp.float32),
        ),
        in_specs=[smem, vmem, vmem, vmem, vmem],
        out_specs=(vmem, vmem),
        scratch_shapes=[pltpu.VMEM((PLANES * kx_local, 2 * width), jnp.float32)],
        compiler_params=pltpu.CompilerParams(vmem_limit_bytes=32 * 1024 * 1024),
    )(slab, arrived, kx_turns, ky_turns, kappa)

    received = lax.all_to_all(moments, "gz", split_axis=0, concat_axis=0, tiled=True)
    return pl.pallas_call(
        far_kernel,
        out_shape=jax.ShapeDtypeStruct((ZDEV, kx_local, width), jnp.float32),
        in_specs=[smem, vmem, vmem, vmem],
        out_specs=vmem,
        scratch_shapes=[pltpu.VMEM((ZDEV, kx_local, width), jnp.float32)],
        compiler_params=pltpu.CompilerParams(vmem_limit_bytes=32 * 1024 * 1024),
    )(slab, near, received, kappa)


def solution(mesh):
    placed = (
        P("gx", "gz", None, None),
        P("gx", "gz", None),
        P("gx", "gz", None, None),
        P("gx", "gz"),
        P(),
        P(),
    )
    return jax.shard_map(
        shards, mesh=mesh, in_specs=placed, out_specs=P("gz", "gx", None), check_vma=False
    )
```

time: 220 us -> 34.8 us (0.16)
  waiting for transfers between devices: 95.5 us -> 5.84 us
  matrix products: 57.1 us -> 0 us
  other arithmetic: 22.2 us -> 1.18 us
  between operations: 13.6 us -> 0.04 us
  starting transfers between devices: 20.3 us -> 7.3 us
  blocking collectives: 0 us -> 10.9 us
  local copies, waits for them, and re-layouts: 10.8 us -> 3.49 us
  Pallas kernels: 0 us -> 5.67 us
    dot_general x8 -> x0, matrix products: 57.1 us -> none  [the longest x1 30.3 us: correlate_terms(): jnp.einsum('abky,bkcy->akcy', green, spec_four, precision=lax.Precision.H...]
    all_gather x1 -> x0, waiting for transfers between devices: 39.8 us -> none  [shards(): piece = lax.all_gather(summed, 'gz', axis=0, tiled=True)]
    reduce_scatter x1 -> x0, waiting for transfers between devices: 24.8 us -> none  [shards(): summed = lax.psum_scatter(spectrum, 'gx', scatter_dimension=1, tiled=True)]
    all_to_all x4 -> x1, waiting for transfers between devices: 19.7 us -> 5.84 us  [shards(): lax.all_to_all(sent, ('gz', 'gx'), split_axis=0, concat_axis=0, tiled=True)]
    dot_general x1 -> x0, other arithmetic: 11.6 us -> none  [correlate_terms(): jnp.einsum('abky,bkcy->akcy', green, spec_four, precision=lax.Precision.H...]
    ppermute x1 -> x0, waiting for transfers between devices: 11.1 us -> none  [shifted(): return lax.ppermute(array, axis, pairs)]
    all_to_all x0 -> x1, blocking collectives: none -> 10.9 us  [shards(): lax.all_to_all(moments, 'gz', split_axis=0, concat_axis=0, tiled=True)]
    all_to_all x4 -> x1, starting transfers between devices: 17.3 us -> 7.3 us  [shards(): lax.all_to_all(sent, ('gz', 'gx'), split_axis=0, concat_axis=0, tiled=True)]
  transfers between devices with their start and end apart: 7 -> 1, of which waited for: 7 -> 1; matrix products, arithmetic and copies ran while one was open for 8% -> 1% of each run, Pallas kernels for 0% -> 0%
where the time goes in v1:
time: 34.8 us; the launch traced here: 34.4 us
  blocking collectives  10.9 us (31%)
  starting transfers between devices  7.3 us (21%)
  waiting for transfers between devices  5.84 us (17%)
  Pallas kernels  5.67 us (16%)
  local copies, waits for them, and re-layouts  3.49 us (10%)
  other arithmetic  1.18 us (3%)
    all_to_all x1, blocking collectives, shards(): lax.all_to_all(moments, 'gz', split_axis=0, concat_axis=0, tiled=True)  10.9 us
    all_to_all x1, starting transfers between devices, shards(): lax.all_to_all(sent, ('gz', 'gx'), split_axis=0, concat_axis=0, tiled=True)  7.3 us
    all_to_all x1, waiting for transfers between devices, shards(): lax.all_to_all(sent, ('gz', 'gx'), split_axis=0, concat_axis=0, tiled=True)  5.84 us
    pallas_call x1, Pallas kernels, shards(): pl.pallas_call(functools.partial(spectrum_kernel, group), out_shape=(jax....  4.87 us
    unnamed x10, local copies, waits for them, and re-layouts  2.69 us
    pallas_call x1, Pallas kernels, shards(): pl.pallas_call(far_kernel, out_shape=jax.ShapeDtypeStruct((ZDEV, kx_local...  0.8 us
    convert_element_type x1, other arithmetic, shards(): place = cells[0].astype(jnp.float32)  0.71 us
  transfers between devices with their start and end apart: 1, of which 1 were waited for; matrix products, arithmetic and copies ran while one was open for 1% of the time, Pallas kernels for 0%

profile of v1, /device:TPU:0, one launch (start us, length us, event | category | flops | bytes accessed | tf_op | source)
XLA Modules:
  0.0 34.4 jit_solution(6108055291394788148)
XLA Ops:
  0.0 0.7 %convert_bitcast_fusion = f32[8,3,64]{2,0,1:T(8,128)S(1)} fusion(s32[1,8,3,64]{3,1,2,0:T(8,128)} %param.8), kind=kLoop, calls=%fused_computation.1 | loop fusion | flops 1536 | bytes 12288 | tf_op jit(solution)/shard_map/convert_element_type | solution.py:204
  0.7 0.0 copy-start
  0.7 0.7 %copy-done = f32[1,8,3,64]{3,1,2,0:T(8,128)S(1)} copy-done((f32[1,8,3,64]{3,1,2,0:T(8,128)S(1)}, f32[1,8,3,64]{3,1,2,0:T(8,128)}, u32[]{:S(2)}) %copy-start) | copy-done | bytes 6168
  1.4 0.0 copy-start.1
  1.4 0.0 copy-start.2
  1.4 0.7 %copy-done.1 = f32[1,8,64]{2,1,0:T(8,128)S(1)} copy-done((f32[1,8,64]{2,1,0:T(8,128)S(1)}, f32[1,8,64]{2,1,0:T(8,128)}, u32[]{:S(2)}) %copy-start.1) | copy-done | bytes 2072
  2.1 0.0 copy-done.2
  2.1 0.1 bitcast_select_fusion
  2.2 0.1 maximum_bitcast_fusion.2
  2.3 0.1 maximum_bitcast_fusion
  2.3 0.6 %broadcast_in_dim.11 = f32[8,4,4,128]{3,2,1,0:T(4,128)} broadcast(f32[8,4,128]{2,1,0:T(4,128)S(1)} %copy.7), dimensions={0,2,3} | broadcast | bytes 81920 | tf_op jit(solution)/shard_map/broadcast_in_dim | solution.py:215
  3.0 7.3 %all-to-all-start = ((f32[32,4,128]{2,1,0:T(4,128)}), f32[32,4,128]{2,1,0:T(4,128)S(1)}, u32[]{:S(2)}, u32[]{:S(2)}) async-start(f32[32,4,128]{2,1,0:T(4,128)} %bitcast.15), calls=%async_computation | async-start | bytes 131072 | tf_op jit(solution)/shard_map/all_to_all | solution.py:216
  10.3 0.0 copy-start.4
  10.3 0.6 %copy-done.4 = s32[64]{0:T(128)S(1)} copy-done((s32[64]{0:T(128)S(1)}, s32[64]{0:T(128)}, u32[]{:S(2)}) %copy-start.4) | copy-done | bytes 280
  11.0 0.1 maximum_multiply_fusion
  11.0 0.0 copy-start.3
  11.0 0.7 %copy-done.3 = s32[64]{0:T(128)S(1)} copy-done((s32[64]{0:T(128)S(1)}, s32[64]{0:T(128)}, u32[]{:S(2)}) %copy-start.3) | copy-done | bytes 280
  11.7 0.1 fusion.1
  11.8 0.1 add_sqrt_fusion.kappa_ref
  11.9 5.8 %all-to-all-done = f32[32,4,128]{2,1,0:T(4,128)S(1)} async-done(((f32[32,4,128]{2,1,0:T(4,128)}), f32[32,4,128]{2,1,0:T(4,128)S(1)}, u32[]{:S(2)}, u32[]{:S(2)}) %all-to-all-start) | async-done | bytes 65568 | tf_op jit(solution)/shard_map/all_to_all | solution.py:216
  17.7 0.1 broadcast_in_dim.12.kx_ref
  17.8 0.1 broadcast_in_dim.13.ky_ref
  17.8 4.9 %shard_map.64 = (f32[32,16,128]{2,1,0:T(8,128)S(1)}, f32[8,3,16,128]{3,2,1,0:T(8,128)S(1)}) custom-call(s32[1]{0:T(128)} %bitcast.slab_ref, f32[128,128]{1,0:T(8,128)S(1)} %bitcast.29, f32[16,128]{1,0:T(8,128)S(1)} %broadcast_in_dim.12.kx_ref, f32[64,128]{1,0:T(8,128)S(1)} %broadcast_in_dim.13.ky_ref, f32[16,128]{1,0:T(8,128)S(1)} %add_sqrt_fusion.kappa_ref), custom_call_target="tpu_custom_call" | custom-call | tf_op jit(solution)/shard_map/pallas_call | solution.py:236
  22.7 10.9 %all_to_all.10.received_ref = f32[8,3,16,128]{3,2,1,0:T(8,128)S(1)} all-to-all(f32[8,3,16,128]{3,2,1,0:T(8,128)S(1)} %get-tuple-element.8), channel_id=1, replica_groups=mesh['gz'=8,'gx'=4] {'gz'}, dimensions={0} | all-to-all | bytes 393216 | tf_op jit(solution)/shard_map/all_to_all | solution.py:248
  33.6 0.8 %shard_map.65 = f32[32,16,128]{2,1,0:T(8,128)} custom-call(s32[1]{0:T(128)} %bitcast.slab_ref, f32[32,16,128]{2,1,0:T(8,128)S(1)} %get-tuple-element.7.near_ref, f32[8,3,16,128]{3,2,1,0:T(8,128)S(1)} %all_to_all.10.received_ref, f32[16,128]{1,0:T(8,128)S(1)} %add_sqrt_fusion.kappa_ref), custom_call_target="tpu_custom_call" | custom-call | tf_op jit(solution)/shard_map/pallas_call | solution.py:249
  (6 shorter events, 0.0 us)
Async XLA Ops:
  0.7 0.7 %copy-start = (f32[1,8,3,64]{3,1,2,0:T(8,128)S(1)}, f32[1,8,3,64]{3,1,2,0:T(8,128)}, u32[]{:S(2)}) copy-start(f32[1,8,3,64]{3,1,2,0:T(8,128)} %param.6) | copy-start | bytes 18436
  1.4 0.7 %copy-start.1 = (f32[1,8,64]{2,1,0:T(8,128)S(1)}, f32[1,8,64]{2,1,0:T(8,128)}, u32[]{:S(2)}) copy-start(f32[1,8,64]{2,1,0:T(8,128)} %param.7) | copy-start | bytes 6148
  1.4 0.7 %copy-start.2 = (s32[1,8]{1,0:T(1,128)S(1)}, s32[1,8]{1,0:T(1,128)}, u32[]{:S(2)}) copy-start(s32[1,8]{1,0:T(1,128)} %param.9) | copy-start | bytes 100
  3.0 14.7 %all-to-all-start = ((f32[32,4,128]{2,1,0:T(4,128)}), f32[32,4,128]{2,1,0:T(4,128)S(1)}, u32[]{:S(2)}, u32[]{:S(2)}) async-start(f32[32,4,128]{2,1,0:T(4,128)} %bitcast.15), calls=%async_computation | async-start | bytes 131072 | tf_op jit(solution)/shard_map/all_to_all | solution.py:216
  10.3 0.7 %copy-start.4 = (s32[64]{0:T(128)S(1)}, s32[64]{0:T(128)}, u32[]{:S(2)}) copy-start(s32[64]{0:T(128)} %param.11) | copy-start | bytes 772
  11.0 0.7 %copy-start.3 = (s32[64]{0:T(128)S(1)}, s32[64]{0:T(128)}, u32[]{:S(2)}) copy-start(s32[64]{0:T(128)} %param.10) | copy-start | bytes 772

commit v2 on v1

v2 whole, which is shorter than its diff:
```python
import functools
import math

import jax
import jax.numpy as jnp
from jax import lax
from jax.experimental import pallas as pl
from jax.experimental.pallas import tpu as pltpu
from jax.sharding import PartitionSpec as P

NXD = 512
ZDEV = 32
SPILL = 3
PLANES = ZDEV + SPILL

SIN_HALF = tuple(math.sqrt(2.0) * c for c in (3.14158202, -5.16714279, 2.54189899, -0.55463611))
COS_HALF = tuple(math.sqrt(2.0) * c for c in (0.9999933, -4.93393801, 4.04128375, -1.22212681))


def poly(u, coefs):
    total = jnp.full_like(u, coefs[-1])
    for c in coefs[-2::-1]:
        total = total * u + c
    return total


def cos_sin_turns(turns):
    r = turns - jnp.round(turns)
    u = r * r
    s = r * poly(u, SIN_HALF)
    return 1.0 - s * s, s * poly(u, COS_HALF)


def node_weights(f):
    g = 1.0 - f
    fg = -0.5 * f * g
    return (
        fg * g,
        1.0 + f * f * (1.5 * f - 2.5),
        1.0 + g * g * (1.5 * g - 2.5),
        fg * f,
    )


def node_phasors(freq):
    return cos_sin_turns(0.5 * freq) + cos_sin_turns(1.5 * freq)


def transform(freq, nodes, middle, pairs):
    c, s = cos_sin_turns(freq * middle)
    c1, s1, c3, s3 = nodes
    even1, odd1, even3, odd3 = pairs
    re = even1 * c1 + even3 * c3
    im = odd1 * s1 + odd3 * s3
    return c * re - s * im, s * re + c * im


def node_pairs(weights):
    w0, w1, w2, w3 = weights
    return w1 + w2, w2 - w1, w0 + w3, w3 - w0


def two_parts(x):
    high = x.astype(jnp.bfloat16)
    return high, (x - high.astype(jnp.float32)).astype(jnp.bfloat16)


def pack_kernel(counts_ref, offsets_ref, strength_ref, cells_ref, sent_ref):
    slabs, cap = strength_ref.shape
    rows = sent_ref.shape[0] // slabs
    slot = lax.broadcasted_iota(jnp.int32, (slabs, cap), 0)
    lane = lax.broadcasted_iota(jnp.int32, (slabs, cap), 1)
    count = jnp.zeros((slabs, cap), jnp.int32)
    for d in range(slabs):
        count = jnp.where(slot == d, counts_ref[0, d], count)
    power = jnp.where(lane < count, strength_ref[...], 0.0)
    for part in range(4):
        if part < 3:
            low, high = offsets_ref[part], cells_ref[part].astype(jnp.float32)
        else:
            low, high = power, jnp.zeros_like(power)
        own = jnp.concatenate([low, high], axis=1)
        far = jnp.concatenate([own[slabs // 2 :], own[: slabs // 2]], axis=0)
        for copy in range(rows // 8):
            sent_ref[pl.ds(copy * 8 + part, slabs, stride=rows), :] = own
            sent_ref[pl.ds(copy * 8 + 4 + part, slabs, stride=rows), :] = far


def partner(index, step, count):
    return index ^ step if count & (count - 1) == 0 else (index + step) % count


def spectrum_kernel(group, slabs, slab_ref, rows_ref, kx_ref, ky_ref, kappa_ref, near_ref, *rest):
    send_refs, (own_ref, far_ref) = rest[:-2], rest[-2:]
    kx_count = kx_ref.shape[0]
    ky_count = ky_ref.shape[0]
    blocks = rows_ref.shape[0] // 16
    kx, ky = kx_ref[...], ky_ref[...]
    kx_nodes, ky_nodes = node_phasors(kx), node_phasors(ky)
    low_lanes = lax.broadcasted_iota(jnp.int32, (8, 128), 1) < 64
    plane = lax.broadcasted_iota(jnp.int32, (40, 128), 0).astype(jnp.float32)

    def operands(frac, cell, weights, row):
        strength = frac[row + 3 : row + 4]
        base_z = cell[row : row + 1]
        middle_x, middle_y = cell[row + 1 : row + 2] + 1.5, cell[row + 2 : row + 3] + 1.5
        wz = [w[row : row + 1] * strength for w in weights]
        wx = node_pairs([w[row + 1 : row + 2] for w in weights])
        wy = node_pairs([w[row + 2 : row + 3].astype(jnp.bfloat16).astype(jnp.float32) for w in weights])
        dist = plane - base_z
        spread = jnp.where(
            dist == 0.0,
            wz[0],
            jnp.where(dist == 1.0, wz[1], jnp.where(dist == 2.0, wz[2], jnp.where(dist == 3.0, wz[3], 0.0))),
        )
        cx, sx = transform(kx, kx_nodes, middle_x, wx)
        cy, sy = transform(ky, ky_nodes, middle_y, wy)
        lhs = []
        for z in range(PLANES):
            here = jnp.broadcast_to(spread[z : z + 1], cx.shape)
            lhs.append(
                jnp.concatenate([(here * cx).astype(jnp.bfloat16), (here * sx).astype(jnp.bfloat16)], axis=1)
            )
        cy_high, cy_low = two_parts(cy)
        sy_high, sy_low = two_parts(-sy)
        rhs = [
            jnp.concatenate(pair, axis=1)
            for pair in ((cy_high, sy_high), (sy_high, -cy_high), (cy_low, sy_low), (sy_low, -cy_low))
        ]
        return jnp.concatenate(lhs, axis=0), jnp.concatenate(rhs, axis=0)

    def one_block(block):
        rows = rows_ref[pl.ds(pl.multiple_of(block * 16, 16), 16), :]
        turned = pltpu.roll(rows, 64, axis=1)
        frac = jnp.where(low_lanes, rows[0:8], turned[8:16])
        cell = jnp.where(low_lanes, turned[0:8], rows[8:16])
        weights = node_weights(frac)
        return operands(frac, cell, weights, 0), operands(frac, cell, weights, 4)

    def step(index, _):
        pieces = [one_block(index * group + j) for j in range(group)]
        for part, acc_ref in enumerate((own_ref, far_ref)):
            lhs = jnp.concatenate([p[part][0] for p in pieces], axis=1)
            rhs = jnp.concatenate([p[part][1] for p in pieces], axis=1)
            product = lax.dot_general(
                lhs, rhs, (((1,), (1,)), ((), ())), preferred_element_type=jnp.float32
            )

            @pl.when(index == 0)
            def _():
                acc_ref[...] = product

            @pl.when(index > 0)
            def _():
                acc_ref[...] += product

        return 0

    lax.fori_loop(0, blocks // group, step, 0)

    half = slabs // 2
    slab = slab_ref[0]
    upper = slab >= half
    first = jnp.where(upper, half, 0)
    member = slab - first
    far_slab = jnp.where(upper, slab - half, slab + half)
    kappa = kappa_ref[...]
    decay = jnp.exp(-kappa)
    width = 2 * ky_count

    def plane_of(acc_ref, z):
        start = z * kx_count
        both = acc_ref[pl.ds(start if isinstance(z, int) else pl.multiple_of(start, kx_count), kx_count), :]
        return both[:, :width] + both[:, width:]

    def spills_of(acc_ref, index):
        inside = jnp.where(index < slabs - 1, 1.0, 0.0)
        return [plane_of(acc_ref, ZDEV + j) * inside for j in range(SPILL)]

    spilled = spills_of(own_ref, slab)
    down = spilled[0] + decay * (spilled[1] + decay * spilled[2])
    for z in range(ZDEV - 1, -1, -1):
        down = decay * down
        near_ref[z] = down
        down = plane_of(own_ref, z) + down
    up = jnp.zeros_like(decay)
    for z in range(ZDEV):
        up = plane_of(own_ref, z) + decay * up
        near_ref[z] += up
    up_near = spilled[0] + decay * up
    up_far = spilled[2] + decay * (spilled[1] + decay * up_near)

    far_spilled = spills_of(far_ref, far_slab)
    moment = jnp.where(
        upper, jnp.zeros_like(decay), far_spilled[0] + decay * (far_spilled[1] + decay * far_spilled[2])
    )
    for j in range(ZDEV):
        moment = plane_of(far_ref, jnp.where(upper, j, ZDEV - 1 - j)) + decay * moment
    far_near = far_spilled[0] + decay * moment
    far_far = far_spilled[2] + decay * (far_spilled[1] + decay * far_near)

    for hop, send_ref in enumerate(send_refs):
        target = first + partner(member, hop, half)
        zero = jnp.zeros_like(decay)
        ahead = target - slab
        reach = jnp.where(
            ahead > 1, ZDEV * ahead - (PLANES - 1), jnp.where(ahead < 0, ZDEV * (-ahead - 1), 0)
        )
        own_weight = jnp.exp(-kappa * reach.astype(jnp.float32))
        own_low = jnp.where(ahead > 0, own_weight * jnp.where(ahead == 1, up_near, up_far), zero)
        own_high = jnp.where(ahead < 0, own_weight * down, zero)
        far_ahead = target - far_slab
        far_reach = jnp.where(
            far_ahead > 1, ZDEV * far_ahead - (PLANES - 1), jnp.where(far_ahead < 0, ZDEV * (-far_ahead - 1), 0)
        )
        far_weight = jnp.exp(-kappa * far_reach.astype(jnp.float32))
        far_low = jnp.where(upper, far_weight * jnp.where(far_ahead == 1, far_near, far_far), zero)
        far_high = jnp.where(upper, zero, far_weight * moment)
        send_ref[0] = own_low + far_low
        send_ref[1] = own_high + far_high
        for j in (1, 2):
            send_ref[1 + j] = jnp.where(
                ahead == 1, spilled[j], jnp.where(far_ahead == 1, far_spilled[j], zero)
            )


def far_kernel(slabs, kappa_ref, near_ref, *rest):
    received_refs, out_ref, powers_ref = rest[:-2], rest[-2], rest[-1]
    kappa = kappa_ref[...]
    decay = jnp.exp(-kappa)
    sigma = 4.0 / (ZDEV * slabs)
    scale = (sigma * 2.0 / NXD) / kappa
    low, high, first, second = (sum(ref[part] for ref in received_refs) * scale for part in range(4))
    for z in range(ZDEV - 1, -1, -1):
        high = decay * high
        powers_ref[z] = high
    extra = {0: decay * (first + decay * second), 1: decay * second}
    source_at = {1: first, 2: second}
    for z in range(ZDEV):
        if z:
            low = decay * low
        if z in source_at:
            low = low + source_at[z]
        total = scale * near_ref[z] + low + powers_ref[z]
        if z in extra:
            total = total + extra[z]
        out_ref[z] = total


def shards(offsets, strength, cells, counts, kx_modes, ky_modes):
    slabs = lax.axis_size("gz")
    x_groups = lax.axis_size("gx")
    half = slabs // 2
    cap = strength.shape[-1]
    slab = lax.axis_index("gz").astype(jnp.int32).reshape(1)

    smem = pl.BlockSpec(memory_space=pltpu.SMEM)
    vmem = pl.BlockSpec(memory_space=pltpu.VMEM)
    sent = pl.pallas_call(
        pack_kernel,
        out_shape=jax.ShapeDtypeStruct((slabs * x_groups * 8, 2 * cap), jnp.float32),
        in_specs=[smem, vmem, vmem, vmem],
        out_specs=vmem,
    )(counts, jnp.transpose(offsets[0], (1, 0, 2)), strength[0], jnp.transpose(cells[0], (1, 0, 2)))
    sent = sent.reshape(slabs * x_groups, 8, 2 * cap)
    arrived = lax.all_to_all(sent, ("gz", "gx"), split_axis=0, concat_axis=0, tiled=True)
    arrived = arrived.reshape(-1, 128)

    kx_local = kx_modes.shape[0] // x_groups
    ky_count = ky_modes.shape[0]
    own_kx = lax.dynamic_slice_in_dim(kx_modes, lax.axis_index("gx") * kx_local, kx_local)
    kx_turns = jnp.broadcast_to((own_kx.astype(jnp.float32) / NXD)[:, None], (kx_local, 128))
    ky_turns = jnp.broadcast_to((ky_modes.astype(jnp.float32) / NXD)[:, None], (ky_count, 128))
    signed_x = jnp.where(own_kx >= NXD // 2, own_kx - NXD, own_kx).astype(jnp.float32)
    signed_y = jnp.where(ky_modes >= NXD // 2, ky_modes - NXD, ky_modes).astype(jnp.float32)
    signed_y = jnp.concatenate([signed_y, signed_y])
    sigma = 4.0 / (ZDEV * slabs)
    step = 2.0 * math.pi / NXD
    kappa = jnp.sqrt(sigma * sigma + step * step * (signed_x[:, None] ** 2 + signed_y[None, :] ** 2))

    width = 2 * ky_count
    blocks = arrived.shape[0] // 16
    group = math.gcd(blocks, 16)
    planes = jax.ShapeDtypeStruct((ZDEV, kx_local, width), jnp.float32)
    message = jax.ShapeDtypeStruct((4, kx_local, width), jnp.float32)
    acc = pltpu.VMEM((PLANES * kx_local, 2 * width), jnp.float32)
    near, *messages = pl.pallas_call(
        functools.partial(spectrum_kernel, group, slabs),
        out_shape=(planes,) + (message,) * half,
        in_specs=[smem, vmem, vmem, vmem, vmem],
        out_specs=(vmem,) * (1 + half),
        scratch_shapes=[acc, acc],
        compiler_params=pltpu.CompilerParams(vmem_limit_bytes=40 * 1024 * 1024),
    )(slab, arrived, kx_turns, ky_turns, kappa)

    received = messages[:1]
    for hop in range(1, half):
        pairs = [(i, i - i % half + partner(i % half, hop, half)) for i in range(slabs)]
        received.append(lax.ppermute(messages[hop], "gz", pairs))
    return pl.pallas_call(
        functools.partial(far_kernel, slabs),
        out_shape=planes,
        in_specs=[vmem] * (2 + half),
        out_specs=vmem,
        scratch_shapes=[pltpu.VMEM((ZDEV, kx_local, width), jnp.float32)],
        compiler_params=pltpu.CompilerParams(vmem_limit_bytes=32 * 1024 * 1024),
    )(kappa, near, *received)


def solution(mesh):
    placed = (
        P("gx", "gz", None, None),
        P("gx", "gz", None),
        P("gx", "gz", None, None),
        P("gx", "gz"),
        P(),
        P(),
    )
    return jax.shard_map(
        shards, mesh=mesh, in_specs=placed, out_specs=P("gz", "gx", None), check_vma=False
    )
```

time: 34.8 us -> 28.5 us (0.82)
  blocking collectives: 10.9 us -> 0 us
  starting transfers between devices: 7.3 us -> 10.8 us
  waiting for transfers between devices: 5.84 us -> 9.3 us
  local copies, waits for them, and re-layouts: 3.49 us -> 1.44 us
  other arithmetic: 1.18 us -> 0.24 us
  Pallas kernels: 5.67 us -> 6.35 us
    all_to_all x1 -> x0, blocking collectives: 10.9 us -> none  [shards(): lax.all_to_all(moments, 'gz', split_axis=0, concat_axis=0, tiled=True)]
    ppermute x0 -> x3, starting transfers between devices: none -> 3.55 us  [shards(): received.append(lax.ppermute(messages[hop], 'gz', pairs))]
    ppermute x0 -> x3, waiting for transfers between devices: none -> 2.63 us  [shards(): received.append(lax.ppermute(messages[hop], 'gz', pairs))]
    unnamed x10 -> x4, local copies, waits for them, and re-layouts: 2.69 us -> 1.3 us
    all_to_all x1, waiting for transfers between devices: 5.84 us -> 6.67 us  [shards(): lax.all_to_all(sent, ('gz', 'gx'), split_axis=0, concat_axis=0, tiled=True)]
    convert_element_type x1 -> x0, other arithmetic: 0.71 us -> none  [shards(): place = cells[0].astype(jnp.float32)]
    pallas_call x2 -> x3, Pallas kernels: 5.67 us -> 6.35 us  [the longest x1 4.01 us: shards(): pl.pallas_call(functools.partial(spectrum_kernel, group, slabs), out_shap...]
    broadcast_in_dim x1 -> x0, local copies, waits for them, and re-layouts: 0.64 us -> none  [shards(): jnp.broadcast_to(rows[:, None], (slabs, x_groups, 4, 128))]
  transfers between devices with their start and end apart: 1 -> 4, of which waited for: 1 -> 4; matrix products, arithmetic and copies ran while one was open for 1% -> 1% of each run, Pallas kernels for 0% -> 0%
where the time goes in v2:
time: 28.5 us; the launch traced here: 28.2 us
  starting transfers between devices  10.8 us (38%)
  waiting for transfers between devices  9.3 us (33%)
  Pallas kernels  6.35 us (22%)
  local copies, waits for them, and re-layouts  1.44 us (5%)
    all_to_all x1, starting transfers between devices, shards(): lax.all_to_all(sent, ('gz', 'gx'), split_axis=0, concat_axis=0, tiled=True)  7.3 us
    all_to_all x1, waiting for transfers between devices, shards(): lax.all_to_all(sent, ('gz', 'gx'), split_axis=0, concat_axis=0, tiled=True)  6.67 us
    pallas_call x1, Pallas kernels, shards(): pl.pallas_call(functools.partial(spectrum_kernel, group, slabs), out_shap...  4.01 us
    ppermute x3, starting transfers between devices, shards(): received.append(lax.ppermute(messages[hop], 'gz', pairs))  3.55 us
    ppermute x3, waiting for transfers between devices, shards(): received.append(lax.ppermute(messages[hop], 'gz', pairs))  2.63 us
    pallas_call x1, Pallas kernels, shards(): pl.pallas_call(pack_kernel, out_shape=jax.ShapeDtypeStruct((slabs * x_gro...  1.58 us
    unnamed x4, local copies, waits for them, and re-layouts  1.3 us
    pallas_call x1, Pallas kernels, shards(): pl.pallas_call(functools.partial(far_kernel, slabs), out_shape=planes, in...  0.77 us
  transfers between devices with their start and end apart: 4, of which 4 were waited for; matrix products, arithmetic and copies ran while one was open for 1% of the time, Pallas kernels for 0%

profile of v2, /device:TPU:0, one launch (start us, length us, event | category | flops | bytes accessed | tf_op | source)
XLA Modules:
  0.0 28.2 jit_solution(4015938805817339299)
XLA Ops:
  0.0 1.6 %shard_map.64 = f32[256,128]{1,0:T(8,128)} custom-call(s32[1,8]{1,0:T(1,128)} %counts_ref.1, f32[3,8,64]{2,1,0:T(8,128)} %bitcast.12, f32[8,64]{1,0:T(8,128)} %bitcast.14, s32[3,8,64]{2,1,0:T(8,128)} %bitcast.13), custom_call_target="tpu_custom_call" | custom-call | tf_op jit(solution)/shard_map/pallas_call | solution.py:259
  1.6 7.3 %all-to-all-start = ((f32[32,8,128]{2,1,0:T(8,128)}), f32[32,8,128]{2,1,0:T(8,128)S(1)}, u32[]{:S(2)}, u32[]{:S(2)}) async-start(f32[32,8,128]{2,1,0:T(8,128)} %bitcast.11), calls=%async_computation | async-start | bytes 262144 | tf_op jit(solution)/shard_map/all_to_all | solution.py:266
  8.9 0.0 copy-start.1
  8.9 0.6 %copy-done.1 = s32[64]{0:T(128)S(1)} copy-done((s32[64]{0:T(128)S(1)}, s32[64]{0:T(128)}, u32[]{:S(2)}) %copy-start.1) | copy-done | bytes 280
  9.6 0.0 copy-start
  9.6 0.7 %copy-done = s32[64]{0:T(128)S(1)} copy-done((s32[64]{0:T(128)S(1)}, s32[64]{0:T(128)}, u32[]{:S(2)}) %copy-start) | copy-done | bytes 280
  10.2 0.1 convert_multiply_fusion.1
  10.3 0.1 maximum_multiply_fusion
  10.4 0.1 add_sqrt_fusion.kappa_ref
  10.4 6.7 %all-to-all-done = f32[32,8,128]{2,1,0:T(8,128)S(1)} async-done(((f32[32,8,128]{2,1,0:T(8,128)}), f32[32,8,128]{2,1,0:T(8,128)S(1)}, u32[]{:S(2)}, u32[]{:S(2)}) %all-to-all-start) | async-done | bytes 131104 | tf_op jit(solution)/shard_map/all_to_all | solution.py:266
  17.1 0.1 broadcast_in_dim.4.kx_ref
  17.2 0.1 broadcast_in_dim.5.ky_ref
  17.3 4.0 %shard_map.65 = (f32[32,16,128]{2,1,0:T(8,128)S(1)}, f32[4,16,128]{2,1,0:T(8,128)S(1)}, f32[4,16,128]{2,1,0:T(8,128)S(1)}, f32[4,16,128]{2,1,0:T(8,128)S(1)}, f32[4,16,128]{2,1,0:T(8,128)S(1)}) custom-call(s32[1]{0:T(128)} %bitcast.slab_ref, f32[256,128]{1,0:T(8,128)S(1)} %bitcast.10, f32[16,128]{1,0:T(8,128)S(1)} %broadcast_in_dim.4.kx_ref, ...), custom_call_target="tpu_custom_call" | custom-call | tf_op jit(solution)/shard_map/pallas_call | solution.py:287
  21.3 0.7 %collective-permute-start = (f32[4,16,128]{2,1,0:T(8,128)S(1)}, f32[4,16,128]{2,1,0:T(8,128)S(1)}, u32[]{:S(2)}, u32[]{:S(2)}) collective-permute-start(f32[4,16,128]{2,1,0:T(8,128)S(1)} %get-tuple-element.12), channel_id=1, source_target_pairs={{0,4},{4,0},{8,12},{12,8},{16,20},{20,16},{24,28},{28,24},{1,5},{5... | collective-permute-start | bytes 98312 | tf_op jit(solution)/shard_map/ppermute | solution.py:299
  22.0 0.7 %collective-permute-start.1 = (f32[4,16,128]{2,1,0:T(8,128)S(1)}, f32[4,16,128]{2,1,0:T(8,128)S(1)}, u32[]{:S(2)}, u32[]{:S(2)}) collective-permute-start(f32[4,16,128]{2,1,0:T(8,128)S(1)} %get-tuple-element.13), channel_id=1, source_target_pairs={{0,8},{4,12},{8,0},{12,4},{16,24},{20,28},{24,16},{28,20},{1,9},{5... | collective-permute-start | bytes 98312 | tf_op jit(solution)/shard_map/ppermute | solution.py:299
  22.6 2.2 %collective-permute-start.2 = (f32[4,16,128]{2,1,0:T(8,128)S(1)}, f32[4,16,128]{2,1,0:T(8,128)S(1)}, u32[]{:S(2)}, u32[]{:S(2)}) collective-permute-start(f32[4,16,128]{2,1,0:T(8,128)S(1)} %get-tuple-element.14), channel_id=1, source_target_pairs={{0,12},{4,8},{8,4},{12,0},{16,28},{20,24},{24,20},{28,16},{1,13},{... | collective-permute-start | bytes 98312 | tf_op jit(solution)/shard_map/ppermute | solution.py:299
  24.8 0.4 %collective-permute-done.rest_1_ = f32[4,16,128]{2,1,0:T(8,128)S(1)} collective-permute-done((f32[4,16,128]{2,1,0:T(8,128)S(1)}, f32[4,16,128]{2,1,0:T(8,128)S(1)}, u32[]{:S(2)}, u32[]{:S(2)}) %collective-permute-start) | collective-permute-done | bytes 32800 | tf_op jit(solution)/shard_map/ppermute | solution.py:299
  25.2 0.8 %collective-permute-done.1.rest_2_ = f32[4,16,128]{2,1,0:T(8,128)S(1)} collective-permute-done((f32[4,16,128]{2,1,0:T(8,128)S(1)}, f32[4,16,128]{2,1,0:T(8,128)S(1)}, u32[]{:S(2)}, u32[]{:S(2)}) %collective-permute-start.1) | collective-permute-done | bytes 32800 | tf_op jit(solution)/shard_map/ppermute | solution.py:299
  26.0 1.4 %collective-permute-done.2.rest_3_ = f32[4,16,128]{2,1,0:T(8,128)S(1)} collective-permute-done((f32[4,16,128]{2,1,0:T(8,128)S(1)}, f32[4,16,128]{2,1,0:T(8,128)S(1)}, u32[]{:S(2)}, u32[]{:S(2)}) %collective-permute-start.2) | collective-permute-done | bytes 32800 | tf_op jit(solution)/shard_map/ppermute | solution.py:299
  27.5 0.8 %shard_map.66 = f32[32,16,128]{2,1,0:T(8,128)} custom-call(f32[16,128]{1,0:T(8,128)S(1)} %add_sqrt_fusion.kappa_ref, f32[32,16,128]{2,1,0:T(8,128)S(1)} %get-tuple-element.10.near_ref, f32[4,16,128]{2,1,0:T(8,128)S(1)} %get-tuple-element.11.rest_0_, f32[4,16,128]{2,1,0:T(8,128)S(1)} %collective-permute-done.rest_1_, ...), custom_call_target="tpu_custom_call" | custom-call | tf_op jit(solution)/shard_map/pallas_call | solution.py:300
  (2 shorter events, 0.0 us)
Async XLA Ops:
  1.6 15.5 %all-to-all-start = ((f32[32,8,128]{2,1,0:T(8,128)}), f32[32,8,128]{2,1,0:T(8,128)S(1)}, u32[]{:S(2)}, u32[]{:S(2)}) async-start(f32[32,8,128]{2,1,0:T(8,128)} %bitcast.11), calls=%async_computation | async-start | bytes 262144 | tf_op jit(solution)/shard_map/all_to_all | solution.py:266
  8.9 0.7 %copy-start.1 = (s32[64]{0:T(128)S(1)}, s32[64]{0:T(128)}, u32[]{:S(2)}) copy-start(s32[64]{0:T(128)} %param.11) | copy-start | bytes 772
  9.6 0.7 %copy-start = (s32[64]{0:T(128)S(1)}, s32[64]{0:T(128)}, u32[]{:S(2)}) copy-start(s32[64]{0:T(128)} %param.10) | copy-start | bytes 772
  21.3 4.0 %collective-permute-start = (f32[4,16,128]{2,1,0:T(8,128)S(1)}, f32[4,16,128]{2,1,0:T(8,128)S(1)}, u32[]{:S(2)}, u32[]{:S(2)}) collective-permute-start(f32[4,16,128]{2,1,0:T(8,128)S(1)} %get-tuple-element.12), channel_id=1, source_target_pairs={{0,4},{4,0},{8,12},{12,8},{16,20},{20,16},{24,28},{28,24},{1,5},{5... | collective-permute-start | bytes 98312 | tf_op jit(solution)/shard_map/ppermute | solution.py:299
  22.0 4.0 %collective-permute-start.1 = (f32[4,16,128]{2,1,0:T(8,128)S(1)}, f32[4,16,128]{2,1,0:T(8,128)S(1)}, u32[]{:S(2)}, u32[]{:S(2)}) collective-permute-start(f32[4,16,128]{2,1,0:T(8,128)S(1)} %get-tuple-element.13), channel_id=1, source_target_pairs={{0,8},{4,12},{8,0},{12,4},{16,24},{20,28},{24,16},{28,20},{1,9},{5... | collective-permute-start | bytes 98312 | tf_op jit(solution)/shard_map/ppermute | solution.py:299
  22.6 4.8 %collective-permute-start.2 = (f32[4,16,128]{2,1,0:T(8,128)S(1)}, f32[4,16,128]{2,1,0:T(8,128)S(1)}, u32[]{:S(2)}, u32[]{:S(2)}) collective-permute-start(f32[4,16,128]{2,1,0:T(8,128)S(1)} %get-tuple-element.14), channel_id=1, source_target_pairs={{0,12},{4,8},{8,4},{12,0},{16,28},{20,24},{24,20},{28,16},{1,13},{... | collective-permute-start | bytes 98312 | tf_op jit(solution)/shard_map/ppermute | solution.py:299

commit v3 on v2

--- a/solution.py
+++ b/solution.py
@@ -12,6 +12,8 @@
 ZDEV = 32
 SPILL = 3
 PLANES = ZDEV + SPILL
+MIDDLE = 126.0
+FINE = 2
 
 SIN_HALF = tuple(math.sqrt(2.0) * c for c in (3.14158202, -5.16714279, 2.54189899, -0.55463611))
 COS_HALF = tuple(math.sqrt(2.0) * c for c in (0.9999933, -4.93393801, 4.04128375, -1.22212681))
@@ -46,8 +48,10 @@
     return cos_sin_turns(0.5 * freq) + cos_sin_turns(1.5 * freq)
 
 
-def transform(freq, nodes, middle, pairs):
-    c, s = cos_sin_turns(freq * middle)
+def transform(table_ref, nodes, column, side, pairs):
+    column = jnp.broadcast_to(column, table_ref.shape[1:])
+    c = jnp.take_along_axis(table_ref[0], column, axis=1)
+    s = jnp.take_along_axis(table_ref[1], column, axis=1) * side
     c1, s1, c3, s3 = nodes
     even1, odd1, even3, odd3 = pairs
     re = even1 * c1 + even3 * c3
@@ -91,19 +95,37 @@
 
 
 def spectrum_kernel(group, slabs, slab_ref, rows_ref, kx_ref, ky_ref, kappa_ref, near_ref, *rest):
-    send_refs, (own_ref, far_ref) = rest[:-2], rest[-2:]
+    send_refs, (own_ref, far_ref, x_table_ref, y_table_ref, fine_table_ref) = (
+        rest[:-5],
+        rest[-5:],
+    )
     kx_count = kx_ref.shape[0]
     ky_count = ky_ref.shape[0]
     blocks = rows_ref.shape[0] // 16
     kx, ky = kx_ref[...], ky_ref[...]
     kx_nodes, ky_nodes = node_phasors(kx), node_phasors(ky)
+    row = lax.broadcasted_iota(jnp.int32, kx.shape, 0).astype(jnp.float32)
+    key = jnp.abs(kx - jnp.round(kx)) * (NXD * kx_count) + row
+    fine_masks, fine = [], []
+    for _ in range(FINE):
+        chosen = key == jnp.min(key, axis=0, keepdims=True)
+        key = jnp.where(chosen, 2.0 * NXD * kx_count, key)
+        fine_masks.append(jnp.where(chosen, 1.0, 0.0))
+        fine.append(jnp.sum(jnp.where(chosen, kx, 0.0), axis=0, keepdims=True))
+    fine_row = lax.broadcasted_iota(jnp.int32, (8, 128), 0)
+    fine = jnp.where((fine_row & 1) == 0, fine[0], fine[1])
+    fine_nodes = node_phasors(fine)
+    columns = lax.broadcasted_iota(jnp.int32, (1, 128), 1).astype(jnp.float32)
+    for freq, table_ref in ((kx, x_table_ref), (ky, y_table_ref), (fine, fine_table_ref)):
+        table_ref[0], table_ref[1] = cos_sin_turns(freq * columns)
     low_lanes = lax.broadcasted_iota(jnp.int32, (8, 128), 1) < 64
     plane = lax.broadcasted_iota(jnp.int32, (40, 128), 0).astype(jnp.float32)
 
-    def operands(frac, cell, weights, row):
+    def operands(frac, cell, column, side, weights, row):
         strength = frac[row + 3 : row + 4]
         base_z = cell[row : row + 1]
-        middle_x, middle_y = cell[row + 1 : row + 2] + 1.5, cell[row + 2 : row + 3] + 1.5
+        column_x, column_y = column[row + 1 : row + 2], column[row + 2 : row + 3]
+        side_x, side_y = side[row + 1 : row + 2], side[row + 2 : row + 3]
         wz = [w[row : row + 1] * strength for w in weights]
         wx = node_pairs([w[row + 1 : row + 2] for w in weights])
         wy = node_pairs([w[row + 2 : row + 3].astype(jnp.bfloat16).astype(jnp.float32) for w in weights])
@@ -113,14 +135,30 @@
             wz[0],
             jnp.where(dist == 1.0, wz[1], jnp.where(dist == 2.0, wz[2], jnp.where(dist == 3.0, wz[3], 0.0))),
         )
-        cx, sx = transform(kx, kx_nodes, middle_x, wx)
-        cy, sy = transform(ky, ky_nodes, middle_y, wy)
+        cx, sx = transform(x_table_ref, kx_nodes, column_x, side_x, wx)
+        cy, sy = transform(y_table_ref, ky_nodes, column_y, side_y, wy)
         lhs = []
         for z in range(PLANES):
             here = jnp.broadcast_to(spread[z : z + 1], cx.shape)
             lhs.append(
                 jnp.concatenate([(here * cx).astype(jnp.bfloat16), (here * sx).astype(jnp.bfloat16)], axis=1)
             )
+        if row == 0:
+            fine_c, fine_s = transform(fine_table_ref, fine_nodes, column_x, side_x, wx)
+            for z in range(0, spread.shape[0], 8):
+                here = [
+                    jnp.take_along_axis(spread[z : z + 8], (fine_row >> 1) + half, axis=0)
+                    for half in range(0, 8, 8 // FINE)
+                ]
+                lhs.append(
+                    jnp.concatenate(
+                        [
+                            two_parts(jnp.concatenate([h * part for h in here], axis=0))[1]
+                            for part in (fine_c, fine_s)
+                        ],
+                        axis=1,
+                    )
+                )
         cy_high, cy_low = two_parts(cy)
         sy_high, sy_low = two_parts(-sy)
         rhs = [
@@ -135,7 +173,9 @@
         frac = jnp.where(low_lanes, rows[0:8], turned[8:16])
         cell = jnp.where(low_lanes, turned[0:8], rows[8:16])
         weights = node_weights(frac)
-        return operands(frac, cell, weights, 0), operands(frac, cell, weights, 4)
+        column = jnp.abs(cell - MIDDLE).astype(jnp.int32)
+        side = jnp.where(cell < MIDDLE, -1.0, 1.0)
+        return tuple(operands(frac, cell, column, side, weights, row) for row in (0, 4))
 
     def step(index, _):
         pieces = [one_block(index * group + j) for j in range(group)]
@@ -171,6 +211,11 @@
     def plane_of(acc_ref, z):
         start = z * kx_count
         both = acc_ref[pl.ds(start if isinstance(z, int) else pl.multiple_of(start, kx_count), kx_count), :]
+        if acc_ref is own_ref:
+            first = PLANES * kx_count + FINE * z
+            for j, mask in enumerate(fine_masks):
+                both_fine = acc_ref[first + j : first + j + 1, :]
+                both = both + jnp.concatenate([mask, mask], axis=1) * both_fine
         return both[:, :width] + both[:, width:]
 
     def spills_of(acc_ref, index):
@@ -224,13 +269,20 @@
             )
 
 
-def far_kernel(slabs, kappa_ref, near_ref, *rest):
+def far_kernel(slabs, kappa_ref, turns_ref, near_ref, *rest):
     received_refs, out_ref, powers_ref = rest[:-2], rest[-2], rest[-1]
     kappa = kappa_ref[...]
     decay = jnp.exp(-kappa)
     sigma = 4.0 / (ZDEV * slabs)
     scale = (sigma * 2.0 / NXD) / kappa
-    low, high, first, second = (sum(ref[part] for ref in received_refs) * scale for part in range(4))
+    width = kappa.shape[1]
+    turn_cos, turn_sin = cos_sin_turns(turns_ref[...])
+    turn_cos = turn_cos * scale
+    turn_sin = turn_sin * scale
+    turn_sin = jnp.where(
+        lax.broadcasted_iota(jnp.int32, kappa.shape, 1) < width // 2, turn_sin, -turn_sin
+    )
+    low, high, first, second = (sum(ref[part] for ref in received_refs) for part in range(4))
     for z in range(ZDEV - 1, -1, -1):
         high = decay * high
         powers_ref[z] = high
@@ -241,10 +293,10 @@
             low = decay * low
         if z in source_at:
             low = low + source_at[z]
-        total = scale * near_ref[z] + low + powers_ref[z]
+        total = near_ref[z] + low + powers_ref[z]
         if z in extra:
             total = total + extra[z]
-        out_ref[z] = total
+        out_ref[z] = turn_cos * total + turn_sin * pltpu.roll(total, width // 2, axis=1)
 
 
 def shards(offsets, strength, cells, counts, kx_modes, ky_modes):
@@ -279,17 +331,26 @@
     kappa = jnp.sqrt(sigma * sigma + step * step * (signed_x[:, None] ** 2 + signed_y[None, :] ** 2))
 
     width = 2 * ky_count
+    both_y = jnp.concatenate([ky_modes, ky_modes])
+    turns = (own_kx[:, None] + both_y[None, :]).astype(jnp.float32) * ((MIDDLE + 1.5) / NXD)
     blocks = arrived.shape[0] // 16
     group = math.gcd(blocks, 16)
     planes = jax.ShapeDtypeStruct((ZDEV, kx_local, width), jnp.float32)
     message = jax.ShapeDtypeStruct((4, kx_local, width), jnp.float32)
-    acc = pltpu.VMEM((PLANES * kx_local, 2 * width), jnp.float32)
+    coarse_rows = PLANES * kx_local
+    fine_rows = FINE * 8 * pl.cdiv(PLANES, 8)
     near, *messages = pl.pallas_call(
         functools.partial(spectrum_kernel, group, slabs),
         out_shape=(planes,) + (message,) * half,
         in_specs=[smem, vmem, vmem, vmem, vmem],
         out_specs=(vmem,) * (1 + half),
-        scratch_shapes=[acc, acc],
+        scratch_shapes=[
+            pltpu.VMEM((coarse_rows + fine_rows, 2 * width), jnp.float32),
+            pltpu.VMEM((coarse_rows, 2 * width), jnp.float32),
+            pltpu.VMEM((2, kx_local, 128), jnp.float32),
+            pltpu.VMEM((2, ky_count, 128), jnp.float32),
+            pltpu.VMEM((2, 8, 128), jnp.float32),
+        ],
         compiler_params=pltpu.CompilerParams(vmem_limit_bytes=40 * 1024 * 1024),
     )(slab, arrived, kx_turns, ky_turns, kappa)
 
@@ -300,11 +361,11 @@
     return pl.pallas_call(
         functools.partial(far_kernel, slabs),
         out_shape=planes,
-        in_specs=[vmem] * (2 + half),
+        in_specs=[vmem] * (3 + half),
         out_specs=vmem,
         scratch_shapes=[pltpu.VMEM((ZDEV, kx_local, width), jnp.float32)],
         compiler_params=pltpu.CompilerParams(vmem_limit_bytes=32 * 1024 * 1024),
-    )(kappa, near, *received)
+    )(kappa, turns, near, *received)
 
 
 def solution(mesh):

time: 28.5 us -> 27.8 us (0.975)
  Pallas kernels: 6.35 us -> 5.74 us
    pallas_call x1, Pallas kernels: 4.01 us -> 3.29 us  [shards(): pl.pallas_call(functools.partial(spectrum_kernel, group, slabs), out_shap...]
where the time goes in v3:
time: 27.8 us; the launch traced here: 27.6 us
  starting transfers between devices  10.8 us (39%)
  waiting for transfers between devices  9.14 us (33%)
  Pallas kernels  5.74 us (21%)
  local copies, waits for them, and re-layouts  1.44 us (5%)
  other arithmetic  0.39 us (1%)
    all_to_all x1, starting transfers between devices, shards(): lax.all_to_all(sent, ('gz', 'gx'), split_axis=0, concat_axis=0, tiled=True)  7.3 us
    all_to_all x1, waiting for transfers between devices, shards(): lax.all_to_all(sent, ('gz', 'gx'), split_axis=0, concat_axis=0, tiled=True)  6.59 us
    ppermute x3, starting transfers between devices, shards(): received.append(lax.ppermute(messages[hop], 'gz', pairs))  3.55 us
    pallas_call x1, Pallas kernels, shards(): pl.pallas_call(functools.partial(spectrum_kernel, group, slabs), out_shap...  3.29 us
    ppermute x3, waiting for transfers between devices, shards(): received.append(lax.ppermute(messages[hop], 'gz', pairs))  2.55 us
    pallas_call x1, Pallas kernels, shards(): pl.pallas_call(pack_kernel, out_shape=jax.ShapeDtypeStruct((slabs * x_gro...  1.58 us
    unnamed x4, local copies, waits for them, and re-layouts  1.3 us
    pallas_call x1, Pallas kernels, shards(): pl.pallas_call(functools.partial(far_kernel, slabs), out_shape=planes, in...  0.87 us
  transfers between devices with their start and end apart: 4, of which 4 were waited for; matrix products, arithmetic and copies ran while one was open for 1% of the time, Pallas kernels for 0%

profile of v3, /device:TPU:0, one launch (start us, length us, event | category | flops | bytes accessed | tf_op | source)
XLA Modules:
  0.0 27.6 jit_solution(5018804852637000270)
XLA Ops:
  0.0 1.6 %shard_map.64 = f32[256,128]{1,0:T(8,128)} custom-call(s32[1,8]{1,0:T(1,128)} %counts_ref.1, f32[3,8,64]{2,1,0:T(8,128)} %bitcast.12, f32[8,64]{1,0:T(8,128)} %bitcast.14, s32[3,8,64]{2,1,0:T(8,128)} %bitcast.13), custom_call_target="tpu_custom_call" | custom-call | tf_op jit(solution)/shard_map/pallas_call | solution.py:311
  1.6 7.3 %all-to-all-start = ((f32[32,8,128]{2,1,0:T(8,128)}), f32[32,8,128]{2,1,0:T(8,128)S(1)}, u32[]{:S(2)}, u32[]{:S(2)}) async-start(f32[32,8,128]{2,1,0:T(8,128)} %bitcast.11), calls=%async_computation | async-start | bytes 262144 | tf_op jit(solution)/shard_map/all_to_all | solution.py:318
  8.9 0.0 copy-start.1
  8.9 0.6 %copy-done.1 = s32[64]{0:T(128)S(1)} copy-done((s32[64]{0:T(128)S(1)}, s32[64]{0:T(128)}, u32[]{:S(2)}) %copy-start.1) | copy-done | bytes 280
  9.6 0.1 pad_add_fusion
  9.6 0.0 copy-start
  9.6 0.7 %copy-done = s32[64]{0:T(128)S(1)} copy-done((s32[64]{0:T(128)S(1)}, s32[64]{0:T(128)}, u32[]{:S(2)}) %copy-start) | copy-done | bytes 280
  10.3 0.1 convert_multiply_fusion.2
  10.4 0.1 maximum_multiply_fusion
  10.4 0.1 add_sqrt_fusion.kappa_ref
  10.5 6.6 %all-to-all-done = f32[32,8,128]{2,1,0:T(8,128)S(1)} async-done(((f32[32,8,128]{2,1,0:T(8,128)}), f32[32,8,128]{2,1,0:T(8,128)S(1)}, u32[]{:S(2)}, u32[]{:S(2)}) %all-to-all-start) | async-done | bytes 131104 | tf_op jit(solution)/shard_map/all_to_all | solution.py:318
  17.1 0.1 broadcast_in_dim.4.kx_ref
  17.2 0.1 broadcast_in_dim.5.ky_ref
  17.3 3.3 %shard_map.65 = (f32[32,16,128]{2,1,0:T(8,128)S(1)}, f32[4,16,128]{2,1,0:T(8,128)S(1)}, f32[4,16,128]{2,1,0:T(8,128)S(1)}, f32[4,16,128]{2,1,0:T(8,128)S(1)}, f32[4,16,128]{2,1,0:T(8,128)S(1)}) custom-call(s32[1]{0:T(128)} %bitcast.slab_ref, f32[256,128]{1,0:T(8,128)S(1)} %bitcast.10, f32[16,128]{1,0:T(8,128)S(1)} %broadcast_in_dim.4.kx_ref, ...), custom_call_target="tpu_custom_call" | custom-call | tf_op jit(solution)/shard_map/pallas_call | solution.py:342
  20.6 0.7 %collective-permute-start = (f32[4,16,128]{2,1,0:T(8,128)S(1)}, f32[4,16,128]{2,1,0:T(8,128)S(1)}, u32[]{:S(2)}, u32[]{:S(2)}) collective-permute-start(f32[4,16,128]{2,1,0:T(8,128)S(1)} %get-tuple-element.12), channel_id=1, source_target_pairs={{0,4},{4,0},{8,12},{12,8},{16,20},{20,16},{24,28},{28,24},{1,5},{5... | collective-permute-start | bytes 98312 | tf_op jit(solution)/shard_map/ppermute | solution.py:360
  21.3 0.6 %collective-permute-start.1 = (f32[4,16,128]{2,1,0:T(8,128)S(1)}, f32[4,16,128]{2,1,0:T(8,128)S(1)}, u32[]{:S(2)}, u32[]{:S(2)}) collective-permute-start(f32[4,16,128]{2,1,0:T(8,128)S(1)} %get-tuple-element.13), channel_id=1, source_target_pairs={{0,8},{4,12},{8,0},{12,4},{16,24},{20,28},{24,16},{28,20},{1,9},{5... | collective-permute-start | bytes 98312 | tf_op jit(solution)/shard_map/ppermute | solution.py:360
  21.9 2.2 %collective-permute-start.2 = (f32[4,16,128]{2,1,0:T(8,128)S(1)}, f32[4,16,128]{2,1,0:T(8,128)S(1)}, u32[]{:S(2)}, u32[]{:S(2)}) collective-permute-start(f32[4,16,128]{2,1,0:T(8,128)S(1)} %get-tuple-element.14), channel_id=1, source_target_pairs={{0,12},{4,8},{8,4},{12,0},{16,28},{20,24},{24,20},{28,16},{1,13},{... | collective-permute-start | bytes 98312 | tf_op jit(solution)/shard_map/ppermute | solution.py:360
  24.1 0.1 convert_multiply_fusion.turns_ref
  24.2 0.4 %collective-permute-done.rest_1_ = f32[4,16,128]{2,1,0:T(8,128)S(1)} collective-permute-done((f32[4,16,128]{2,1,0:T(8,128)S(1)}, f32[4,16,128]{2,1,0:T(8,128)S(1)}, u32[]{:S(2)}, u32[]{:S(2)}) %collective-permute-start) | collective-permute-done | bytes 32800 | tf_op jit(solution)/shard_map/ppermute | solution.py:360
  24.5 0.8 %collective-permute-done.1.rest_2_ = f32[4,16,128]{2,1,0:T(8,128)S(1)} collective-permute-done((f32[4,16,128]{2,1,0:T(8,128)S(1)}, f32[4,16,128]{2,1,0:T(8,128)S(1)}, u32[]{:S(2)}, u32[]{:S(2)}) %collective-permute-start.1) | collective-permute-done | bytes 32800 | tf_op jit(solution)/shard_map/ppermute | solution.py:360
  25.3 1.4 %collective-permute-done.2.rest_3_ = f32[4,16,128]{2,1,0:T(8,128)S(1)} collective-permute-done((f32[4,16,128]{2,1,0:T(8,128)S(1)}, f32[4,16,128]{2,1,0:T(8,128)S(1)}, u32[]{:S(2)}, u32[]{:S(2)}) %collective-permute-start.2) | collective-permute-done | bytes 32800 | tf_op jit(solution)/shard_map/ppermute | solution.py:360
  26.7 0.9 %shard_map.66 = f32[32,16,128]{2,1,0:T(8,128)} custom-call(f32[16,128]{1,0:T(8,128)S(1)} %add_sqrt_fusion.kappa_ref, f32[16,128]{1,0:T(8,128)S(1)} %convert_multiply_fusion.turns_ref, f32[32,16,128]{2,1,0:T(8,128)S(1)} %get-tuple-element.10.near_ref, f32[4,16,128]{2,1,0:T(8,128)S(1)} %get-tuple-element.11.rest_0_, ...), custom_call_target="tpu_custom_call" | custom-call | tf_op jit(solution)/shard_map/pallas_call | solution.py:361
  (3 shorter events, 0.0 us)
Async XLA Ops:
  1.6 15.5 %all-to-all-start = ((f32[32,8,128]{2,1,0:T(8,128)}), f32[32,8,128]{2,1,0:T(8,128)S(1)}, u32[]{:S(2)}, u32[]{:S(2)}) async-start(f32[32,8,128]{2,1,0:T(8,128)} %bitcast.11), calls=%async_computation | async-start | bytes 262144 | tf_op jit(solution)/shard_map/all_to_all | solution.py:318
  8.9 0.7 %copy-start.1 = (s32[64]{0:T(128)S(1)}, s32[64]{0:T(128)}, u32[]{:S(2)}) copy-start(s32[64]{0:T(128)} %param.11) | copy-start | bytes 772
  9.6 0.7 %copy-start = (s32[64]{0:T(128)S(1)}, s32[64]{0:T(128)}, u32[]{:S(2)}) copy-start(s32[64]{0:T(128)} %param.10) | copy-start | bytes 772
  20.6 4.0 %collective-permute-start = (f32[4,16,128]{2,1,0:T(8,128)S(1)}, f32[4,16,128]{2,1,0:T(8,128)S(1)}, u32[]{:S(2)}, u32[]{:S(2)}) collective-permute-start(f32[4,16,128]{2,1,0:T(8,128)S(1)} %get-tuple-element.12), channel_id=1, source_target_pairs={{0,4},{4,0},{8,12},{12,8},{16,20},{20,16},{24,28},{28,24},{1,5},{5... | collective-permute-start | bytes 98312 | tf_op jit(solution)/shard_map/ppermute | solution.py:360
  21.3 4.0 %collective-permute-start.1 = (f32[4,16,128]{2,1,0:T(8,128)S(1)}, f32[4,16,128]{2,1,0:T(8,128)S(1)}, u32[]{:S(2)}, u32[]{:S(2)}) collective-permute-start(f32[4,16,128]{2,1,0:T(8,128)S(1)} %get-tuple-element.13), channel_id=1, source_target_pairs={{0,8},{4,12},{8,0},{12,4},{16,24},{20,28},{24,16},{28,20},{1,9},{5... | collective-permute-start | bytes 98312 | tf_op jit(solution)/shard_map/ppermute | solution.py:360
  21.9 4.8 %collective-permute-start.2 = (f32[4,16,128]{2,1,0:T(8,128)S(1)}, f32[4,16,128]{2,1,0:T(8,128)S(1)}, u32[]{:S(2)}, u32[]{:S(2)}) collective-permute-start(f32[4,16,128]{2,1,0:T(8,128)S(1)} %get-tuple-element.14), channel_id=1, source_target_pairs={{0,12},{4,8},{8,4},{12,0},{16,28},{20,24},{24,20},{28,16},{1,13},{... | collective-permute-start | bytes 98312 | tf_op jit(solution)/shard_map/ppermute | solution.py:360

commit v4 on v3

v4 whole, which is shorter than its diff:
```python
import functools
import math

import jax
import jax.numpy as jnp
from jax import lax
from jax.experimental import pallas as pl
from jax.experimental.pallas import tpu as pltpu
from jax.sharding import PartitionSpec as P

NXD = 512
ZDEV = 32
SPILL = 3
PLANES = ZDEV + SPILL
MIDDLE = 126.0
FINE = 2

SIN_HALF = tuple(math.sqrt(2.0) * c for c in (3.14158202, -5.16714279, 2.54189899, -0.55463611))
COS_HALF = tuple(math.sqrt(2.0) * c for c in (0.9999933, -4.93393801, 4.04128375, -1.22212681))


def poly(u, coefs):
    total = jnp.full_like(u, coefs[-1])
    for c in coefs[-2::-1]:
        total = total * u + c
    return total


def cos_sin_turns(turns):
    r = turns - jnp.round(turns)
    u = r * r
    s = r * poly(u, SIN_HALF)
    return 1.0 - s * s, s * poly(u, COS_HALF)


def node_weights(f):
    g = 1.0 - f
    fg = -0.5 * f * g
    return (
        fg * g,
        1.0 + f * f * (1.5 * f - 2.5),
        1.0 + g * g * (1.5 * g - 2.5),
        fg * f,
    )


def node_phasors(freq):
    return cos_sin_turns(0.5 * freq) + cos_sin_turns(1.5 * freq)


def transform(table_ref, column, side, pairs):
    column = jnp.broadcast_to(column, table_ref.shape[1:])
    c = jnp.take_along_axis(table_ref[0], column, axis=1)
    s = jnp.take_along_axis(table_ref[1], column, axis=1) * side
    even1, odd1, even3, odd3 = pairs
    re = even1 * table_ref[2] + even3 * table_ref[4]
    im = odd1 * table_ref[3] + odd3 * table_ref[5]
    return c * re - s * im, s * re + c * im


def node_pairs(weights):
    w0, w1, w2, w3 = weights
    return w1 + w2, w2 - w1, w0 + w3, w3 - w0


def two_parts(x):
    high = x.astype(jnp.bfloat16)
    return high, (x - high.astype(jnp.float32)).astype(jnp.bfloat16)


def partner(index, step, count):
    return index ^ step if count & (count - 1) == 0 else (index + step) % count


def pack_rows(counts_ref, offsets_ref, strength_ref, cells_ref, sent_ref):
    slabs, cap = strength_ref.shape
    slot = lax.broadcasted_iota(jnp.int32, (slabs, cap), 0)
    lane = lax.broadcasted_iota(jnp.int32, (slabs, cap), 1)
    count = jnp.zeros((slabs, cap), jnp.int32)
    for d in range(slabs):
        count = jnp.where(slot == d, counts_ref[0, d], count)
    power = jnp.where(lane < count, strength_ref[...], 0.0)
    for part in range(4):
        if part < 3:
            low, high = offsets_ref[part], cells_ref[part].astype(jnp.float32)
        else:
            low, high = power, jnp.zeros_like(power)
        own = jnp.concatenate([low, high], axis=1)
        far = jnp.concatenate([own[slabs // 2 :], own[: slabs // 2]], axis=0)
        for first in range(0, sent_ref.shape[0], 8 * slabs):
            sent_ref[pl.ds(first + part, slabs, stride=8), :] = own
            sent_ref[pl.ds(first + 4 + part, slabs, stride=8), :] = far


def prepare_kernel(
    slabs, slab_ref, x_group_ref, counts_ref, offsets_ref, strength_ref, cells_ref, kx_modes_ref, ky_modes_ref,
    sent_ref, x_ref, y_ref, fine_ref, mask_ref, power_ref, weight_ref, turn_ref,
):
    pack_rows(counts_ref, offsets_ref, strength_ref, cells_ref, sent_ref)

    slab, x_group = slab_ref[0], x_group_ref[0]
    kx_count, ky_count = x_ref.shape[1], y_ref.shape[1]

    def down_rows(modes, rows, first):
        lane = lax.broadcasted_iota(jnp.int32, (rows, modes.shape[1]), 1)
        row = lax.broadcasted_iota(jnp.int32, (rows, modes.shape[1]), 0)
        picked = jnp.sum(jnp.where(lane == row + first, modes, 0.0), axis=1, keepdims=True)
        return jnp.broadcast_to(picked, (rows, 128))

    ky_modes = ky_modes_ref[...].astype(jnp.float32)
    kx_rows = down_rows(kx_modes_ref[...].astype(jnp.float32), kx_count, x_group * kx_count)
    ky_rows = down_rows(ky_modes, ky_count, 0)
    ky_lanes = jnp.concatenate([ky_modes, ky_modes], axis=1)
    kx, ky = kx_rows * (1.0 / NXD), ky_rows * (1.0 / NXD)
    sigma = 4.0 / (ZDEV * slabs)
    step = 2.0 * math.pi / NXD
    signed_x = jnp.where(kx_rows >= NXD // 2, kx_rows - NXD, kx_rows)
    signed_y = jnp.where(ky_lanes >= NXD // 2, ky_lanes - NXD, ky_lanes)
    kappa = jnp.sqrt(sigma * sigma + step * step * (signed_x * signed_x + signed_y * signed_y))
    turns = (kx_rows + ky_lanes) * ((MIDDLE + 1.5) / NXD)

    row = lax.broadcasted_iota(jnp.int32, kx.shape, 0).astype(jnp.float32)
    key = jnp.abs(kx - jnp.round(kx)) * (NXD * kx_count) + row
    fine = []
    for j in range(FINE):
        chosen = key == jnp.min(key, axis=0, keepdims=True)
        key = jnp.where(chosen, 2.0 * NXD * kx_count, key)
        mask_ref[j] = jnp.where(chosen, 1.0, 0.0)
        fine.append(jnp.sum(jnp.where(chosen, kx, 0.0), axis=0, keepdims=True))
    fine_row = lax.broadcasted_iota(jnp.int32, (8, 128), 0)
    fine = jnp.where((fine_row & 1) == 0, fine[0], fine[1])

    columns = lax.broadcasted_iota(jnp.int32, (1, 128), 1).astype(jnp.float32)
    for freq, table_ref in ((kx, x_ref), (ky, y_ref), (fine, fine_ref)):
        for j, part in enumerate(cos_sin_turns(freq * columns) + node_phasors(freq)):
            table_ref[j] = part

    decay = jnp.exp(-kappa)
    power = jnp.ones_like(kappa)
    for z in range(ZDEV + 1):
        power_ref[z] = power
        power = power * decay

    half = slabs // 2
    first = jnp.where(slab >= half, half, 0)
    far_slab = jnp.where(slab >= half, slab - half, slab + half)
    for hop in range(half):
        target = first + partner(slab - first, hop, half)
        for j, source in enumerate((slab, far_slab)):
            ahead = target - source
            reach = jnp.where(
                ahead > 1, ZDEV * ahead - (PLANES - 1), jnp.where(ahead < 0, ZDEV * (-ahead - 1), 0)
            )
            weight_ref[2 * hop + j] = jnp.exp(-kappa * reach.astype(jnp.float32))

    scale = (sigma * 2.0 / NXD) / kappa
    turn_cos, turn_sin = cos_sin_turns(turns)
    real = lax.broadcasted_iota(jnp.int32, kappa.shape, 1) < kappa.shape[1] // 2
    turn_ref[0] = scale * turn_cos
    turn_ref[1] = scale * jnp.where(real, turn_sin, -turn_sin)


def spectrum_kernel(
    group, slabs, slab_ref, rows_ref, x_ref, y_ref, fine_ref, mask_ref, power_ref, weight_ref, near_ref, *rest
):
    send_refs, (own_ref, far_ref) = rest[:-2], rest[-2:]
    kx_count = x_ref.shape[1]
    ky_count = y_ref.shape[1]
    blocks = rows_ref.shape[0] // 16
    low_lanes = lax.broadcasted_iota(jnp.int32, (8, 128), 1) < 64
    plane = lax.broadcasted_iota(jnp.int32, (40, 128), 0).astype(jnp.float32)
    fine_row = lax.broadcasted_iota(jnp.int32, (8, 128), 0)

    def operands(frac, cell, column, side, weights, row):
        strength = frac[row + 3 : row + 4]
        base_z = cell[row : row + 1]
        column_x, column_y = column[row + 1 : row + 2], column[row + 2 : row + 3]
        side_x, side_y = side[row + 1 : row + 2], side[row + 2 : row + 3]
        wz = [w[row : row + 1] * strength for w in weights]
        wx = node_pairs([w[row + 1 : row + 2] for w in weights])
        wy = node_pairs([w[row + 2 : row + 3].astype(jnp.bfloat16).astype(jnp.float32) for w in weights])
        dist = plane - base_z
        spread = jnp.where(
            dist == 0.0,
            wz[0],
            jnp.where(dist == 1.0, wz[1], jnp.where(dist == 2.0, wz[2], jnp.where(dist == 3.0, wz[3], 0.0))),
        )
        cx, sx = transform(x_ref, column_x, side_x, wx)
        cy, sy = transform(y_ref, column_y, side_y, wy)
        lhs = []
        for z in range(PLANES):
            here = jnp.broadcast_to(spread[z : z + 1], cx.shape)
            lhs.append(
                jnp.concatenate([(here * cx).astype(jnp.bfloat16), (here * sx).astype(jnp.bfloat16)], axis=1)
            )
        if row == 0:
            fine_c, fine_s = transform(fine_ref, column_x, side_x, wx)
            for z in range(0, spread.shape[0], 8):
                here = [
                    jnp.take_along_axis(spread[z : z + 8], (fine_row >> 1) + half, axis=0)
                    for half in range(0, 8, 8 // FINE)
                ]
                lhs.append(
                    jnp.concatenate(
                        [
                            two_parts(jnp.concatenate([h * part for h in here], axis=0))[1]
                            for part in (fine_c, fine_s)
                        ],
                        axis=1,
                    )
                )
        cy_high, cy_low = two_parts(cy)
        sy_high, sy_low = two_parts(-sy)
        rhs = [
            jnp.concatenate(pair, axis=1)
            for pair in ((cy_high, sy_high), (sy_high, -cy_high), (cy_low, sy_low), (sy_low, -cy_low))
        ]
        return jnp.concatenate(lhs, axis=0), jnp.concatenate(rhs, axis=0)

    def one_block(block):
        rows = rows_ref[pl.ds(pl.multiple_of(block * 16, 16), 16), :]
        turned = pltpu.roll(rows, 64, axis=1)
        frac = jnp.where(low_lanes, rows[0:8], turned[8:16])
        cell = jnp.where(low_lanes, turned[0:8], rows[8:16])
        weights = node_weights(frac)
        column = jnp.abs(cell - MIDDLE).astype(jnp.int32)
        side = jnp.where(cell < MIDDLE, -1.0, 1.0)
        return tuple(operands(frac, cell, column, side, weights, row) for row in (0, 4))

    def step(index, _):
        pieces = [one_block(index * group + j) for j in range(group)]
        for part, acc_ref in enumerate((own_ref, far_ref)):
            lhs = jnp.concatenate([p[part][0] for p in pieces], axis=1)
            rhs = jnp.concatenate([p[part][1] for p in pieces], axis=1)
            product = lax.dot_general(
                lhs, rhs, (((1,), (1,)), ((), ())), preferred_element_type=jnp.float32
            )

            @pl.when(index == 0)
            def _():
                acc_ref[...] = product

            @pl.when(index > 0)
            def _():
                acc_ref[...] += product

        return 0

    lax.fori_loop(0, blocks // group, step, 0)

    half = slabs // 2
    slab = slab_ref[0]
    upper = slab >= half
    first = jnp.where(upper, half, 0)
    member = slab - first
    far_slab = jnp.where(upper, slab - half, slab + half)
    decay = power_ref[1]
    width = 2 * ky_count

    def plane_of(acc_ref, z):
        start = z * kx_count
        both = acc_ref[pl.ds(start if isinstance(z, int) else pl.multiple_of(start, kx_count), kx_count), :]
        plane = both[:, :width] + both[:, width:]
        if acc_ref is own_ref:
            first = PLANES * kx_count + FINE * z
            for j in range(FINE):
                plane = plane + mask_ref[j] * acc_ref[first + j : first + j + 1, :width]
        return plane

    def spills_of(acc_ref, index):
        inside = jnp.where(index < slabs - 1, 1.0, 0.0)
        return [plane_of(acc_ref, ZDEV + j) * inside for j in range(SPILL)]

    spilled = spills_of(own_ref, slab)
    down = spilled[0] + decay * (spilled[1] + decay * spilled[2])
    for z in range(ZDEV - 1, -1, -1):
        down = decay * down
        near_ref[z] = down
        down = plane_of(own_ref, z) + down
    up = jnp.zeros_like(decay)
    for z in range(ZDEV):
        up = plane_of(own_ref, z) + decay * up
        near_ref[z] += up
    up_near = spilled[0] + decay * up
    up_far = spilled[2] + decay * (spilled[1] + decay * up_near)

    far_spilled = spills_of(far_ref, far_slab)
    moment = jnp.where(
        upper, jnp.zeros_like(decay), far_spilled[0] + decay * (far_spilled[1] + decay * far_spilled[2])
    )
    for j in range(ZDEV):
        moment = plane_of(far_ref, jnp.where(upper, j, ZDEV - 1 - j)) + decay * moment
    far_near = far_spilled[0] + decay * moment
    far_far = far_spilled[2] + decay * (far_spilled[1] + decay * far_near)

    for hop, send_ref in enumerate(send_refs):
        target = first + partner(member, hop, half)
        zero = jnp.zeros_like(decay)
        ahead = target - slab
        own_weight = weight_ref[2 * hop]
        own_low = jnp.where(ahead > 0, own_weight * jnp.where(ahead == 1, up_near, up_far), zero)
        own_high = jnp.where(ahead < 0, own_weight * down, zero)
        far_ahead = target - far_slab
        far_weight = weight_ref[2 * hop + 1]
        far_low = jnp.where(upper, far_weight * jnp.where(far_ahead == 1, far_near, far_far), zero)
        far_high = jnp.where(upper, zero, far_weight * moment)
        send_ref[0] = own_low + far_low
        send_ref[1] = own_high + far_high
        for j in (1, 2):
            send_ref[1 + j] = jnp.where(
                ahead == 1, spilled[j], jnp.where(far_ahead == 1, far_spilled[j], zero)
            )


def far_kernel(power_ref, turn_ref, near_ref, *rest):
    received_refs, out_ref = rest[:-1], rest[-1]
    low, high, first, second = (sum(ref[part] for ref in received_refs) for part in range(4))
    decay = power_ref[1]
    turn_cos, turn_sin = turn_ref[0], turn_ref[1]
    low_at = [
        low + decay * (first + decay * second),
        decay * low + first + decay * second,
        decay * (decay * low + first) + second,
    ]
    for z in range(ZDEV):
        total = near_ref[z] + power_ref[ZDEV - z] * high
        total = total + (low_at[z] if z < 3 else power_ref[z - 2] * low_at[2])
        out_ref[z] = turn_cos * total + turn_sin * pltpu.roll(total, total.shape[1] // 2, axis=1)


def shards(offsets, strength, cells, counts, kx_modes, ky_modes):
    slabs = lax.axis_size("gz")
    x_groups = lax.axis_size("gx")
    half = slabs // 2
    cap = strength.shape[-1]
    kx_local = kx_modes.shape[0] // x_groups
    ky_count = ky_modes.shape[0]
    width = 2 * ky_count
    slab = lax.axis_index("gz").astype(jnp.int32).reshape(1)
    x_group = lax.axis_index("gx").astype(jnp.int32).reshape(1)

    smem = pl.BlockSpec(memory_space=pltpu.SMEM)
    vmem = pl.BlockSpec(memory_space=pltpu.VMEM)
    some = 16 * 1024 * 1024

    def shaped(*shape):
        return jax.ShapeDtypeStruct(shape, jnp.float32)

    prepared = (
        shaped(slabs * x_groups * 8, 2 * cap),
        shaped(6, kx_local, 128),
        shaped(6, ky_count, 128),
        shaped(6, 8, 128),
        shaped(FINE, kx_local, width),
        shaped(ZDEV + 1, kx_local, width),
        shaped(2 * half, kx_local, width),
        shaped(2, kx_local, width),
    )
    inputs = (
        jnp.transpose(offsets[0], (1, 0, 2)),
        strength[0],
        jnp.transpose(cells[0], (1, 0, 2)),
        kx_modes.reshape(1, -1),
        ky_modes.reshape(1, -1),
    )
    sent, *tables, turn = pl.pallas_call(
        functools.partial(prepare_kernel, slabs),
        out_shape=prepared,
        in_specs=[smem] * 3 + [vmem] * len(inputs),
        out_specs=(vmem,) * len(prepared),
        compiler_params=pltpu.CompilerParams(vmem_limit_bytes=some),
    )(slab, x_group, *(pltpu.with_memory_space_constraint(array, pltpu.HBM) for array in (counts,) + inputs))
    powers = tables[4]
    sent = sent.reshape(slabs * x_groups, 8, 2 * cap)
    arrived = lax.all_to_all(sent, ("gx", "gz"), split_axis=0, concat_axis=0, tiled=True)
    arrived = arrived.reshape(-1, 128)

    blocks = arrived.shape[0] // 16
    group = math.gcd(blocks, 16)
    planes = shaped(ZDEV, kx_local, width)
    message = shaped(4, kx_local, width)
    coarse_rows = PLANES * kx_local
    fine_rows = FINE * 8 * pl.cdiv(PLANES, 8)
    near, *messages = pl.pallas_call(
        functools.partial(spectrum_kernel, group, slabs),
        out_shape=(planes,) + (message,) * half,
        in_specs=[smem] + [vmem] * (1 + len(tables)),
        out_specs=(vmem,) * (1 + half),
        scratch_shapes=[
            pltpu.VMEM((coarse_rows + fine_rows, 2 * width), jnp.float32),
            pltpu.VMEM((coarse_rows, 2 * width), jnp.float32),
        ],
        compiler_params=pltpu.CompilerParams(vmem_limit_bytes=40 * 1024 * 1024),
    )(slab, arrived, *tables)

    received = messages[:1]
    for hop in range(1, half):
        pairs = [(i, i - i % half + partner(i % half, hop, half)) for i in range(slabs)]
        received.append(lax.ppermute(messages[hop], "gz", pairs))
    return pl.pallas_call(
        far_kernel,
        out_shape=planes,
        in_specs=[vmem] * (3 + half),
        out_specs=vmem,
        compiler_params=pltpu.CompilerParams(vmem_limit_bytes=some),
    )(powers, turn, near, *received)


def solution(mesh):
    placed = (
        P("gx", "gz", None, None),
        P("gx", "gz", None),
        P("gx", "gz", None, None),
        P("gx", "gz"),
        P(),
        P(),
    )
    return jax.shard_map(
        shards, mesh=mesh, in_specs=placed, out_specs=P("gz", "gx", None), check_vma=False
    )
```

time: 27.8 us -> 27 us (0.971)
  blocking collectives: 0 us -> 14.8 us
  starting transfers between devices: 10.8 us -> 3.55 us
  waiting for transfers between devices: 9.14 us -> 3.22 us
  local copies, waits for them, and re-layouts: 1.44 us -> 0 us
  Pallas kernels: 5.74 us -> 5.23 us
  other arithmetic: 0.39 us -> 0 us
    all_to_all x0 -> x1, blocking collectives: none -> 14.8 us  [shards(): lax.all_to_all(sent, ('gx', 'gz'), split_axis=0, concat_axis=0, tiled=True)]
    all_to_all x1 -> x0, starting transfers between devices: 7.3 us -> none  [shards(): lax.all_to_all(sent, ('gz', 'gx'), split_axis=0, concat_axis=0, tiled=True)]
    all_to_all x1 -> x0, waiting for transfers between devices: 6.59 us -> none  [shards(): lax.all_to_all(sent, ('gz', 'gx'), split_axis=0, concat_axis=0, tiled=True)]
    unnamed x4 -> x0, local copies, waits for them, and re-layouts: 1.3 us -> none
    ppermute x3, waiting for transfers between devices: 2.55 us -> 3.22 us  [shards(): received.append(lax.ppermute(messages[hop], 'gz', pairs))]
    pallas_call x2, Pallas kernels: 2.45 us -> 1.88 us  [the longest x1 1.02 us: shards(): pl.pallas_call(functools.partial(prepare_kernel, slabs), out_shape=prepar...]
  transfers between devices with their start and end apart: 4 -> 3, of which waited for: 4 -> 3; matrix products, arithmetic and copies ran while one was open for 1% -> 0% of each run, Pallas kernels for 0% -> 0%
where the time goes in v4:
time: 27 us; the launch traced here: 26.9 us
  blocking collectives  14.8 us (55%)
  Pallas kernels  5.23 us (19%)
  starting transfers between devices  3.55 us (13%)
  waiting for transfers between devices  3.22 us (12%)
    all_to_all x1, blocking collectives, shards(): lax.all_to_all(sent, ('gx', 'gz'), split_axis=0, concat_axis=0, tiled=True)  14.8 us
    ppermute x3, starting transfers between devices, shards(): received.append(lax.ppermute(messages[hop], 'gz', pairs))  3.55 us
    pallas_call x1, Pallas kernels, shards(): pl.pallas_call(functools.partial(spectrum_kernel, group, slabs), out_shap...  3.36 us
    ppermute x3, waiting for transfers between devices, shards(): received.append(lax.ppermute(messages[hop], 'gz', pairs))  3.22 us
    pallas_call x1, Pallas kernels, shards(): pl.pallas_call(functools.partial(prepare_kernel, slabs), out_shape=prepar...  1.02 us
    pallas_call x1, Pallas kernels, shards(): pl.pallas_call(far_kernel, out_shape=planes, in_specs=[vmem] * (3 + half)...  0.86 us
  transfers between devices with their start and end apart: 3, of which 3 were waited for; matrix products, arithmetic and copies ran while one was open for 0% of the time, Pallas kernels for 0%

profile of v4, /device:TPU:0, one launch (start us, length us, event | category | flops | bytes accessed | tf_op | source)
XLA Modules:
  0.0 26.9 jit_solution(14907234599582383944)
XLA Ops:
  0.0 1.0 %shard_map.64 = (f32[256,128]{1,0:T(8,128)S(1)}, f32[6,16,128]{2,1,0:T(8,128)S(1)}, f32[6,64,128]{2,1,0:T(8,128)S(1)}, f32[6,8,128]{2,1,0:T(8,128)S(1)}, f32[2,1...) custom-call(s32[1]{0:T(128)} %bitcast.slab_ref, ...), custom_call_target="tpu_custom_call" | custom-call | tf_op jit(solution)/shard_map/pallas_call | solution.py:366
  1.0 14.8 %all_to_all.5 = f32[32,8,128]{2,1,0:T(8,128)S(1)} all-to-all(f32[32,8,128]{2,1,0:T(8,128)S(1)} %bitcast.14), channel_id=1, replica_groups=mesh['gz'=8,'gx'=4] {'gx','gz'}, dimensions={0} | all-to-all | bytes 262144 | tf_op jit(solution)/shard_map/all_to_all | solution.py:375
  15.9 3.4 %shard_map.65 = (f32[32,16,128]{2,1,0:T(8,128)S(1)}, f32[4,16,128]{2,1,0:T(8,128)S(1)}, f32[4,16,128]{2,1,0:T(8,128)S(1)}, f32[4,16,128]{2,1,0:T(8,128)S(1)}, f32[4,16,128]{2,1,0:T(8,128)S(1)}) custom-call(s32[1]{0:T(128)} %bitcast.slab_ref, f32[256,128]{1,0:T(8,128)S(1)} %bitcast.13, f32[6,16,128]{2,1,0:T(8,128)S(1)} %get-tuple-element.21.x_ref, ...), custom_call_target="tpu_custom_call" | custom-call | tf_op jit(solution)/shard_map/pallas_call | solution.py:384
  19.2 1.3 %collective-permute-start = (f32[4,16,128]{2,1,0:T(8,128)S(1)}, f32[4,16,128]{2,1,0:T(8,128)S(1)}, u32[]{:S(2)}, u32[]{:S(2)}) collective-permute-start(f32[4,16,128]{2,1,0:T(8,128)S(1)} %get-tuple-element.28), channel_id=1, source_target_pairs={{0,4},{4,0},{8,12},{12,8},{16,20},{20,16},{24,28},{28,24},{1,5},{5... | collective-permute-start | bytes 98312 | tf_op jit(solution)/shard_map/ppermute | solution.py:399
  20.5 0.7 %collective-permute-start.1 = (f32[4,16,128]{2,1,0:T(8,128)S(1)}, f32[4,16,128]{2,1,0:T(8,128)S(1)}, u32[]{:S(2)}, u32[]{:S(2)}) collective-permute-start(f32[4,16,128]{2,1,0:T(8,128)S(1)} %get-tuple-element.29), channel_id=1, source_target_pairs={{0,8},{4,12},{8,0},{12,4},{16,24},{20,28},{24,16},{28,20},{1,9},{5... | collective-permute-start | bytes 98312 | tf_op jit(solution)/shard_map/ppermute | solution.py:399
  21.2 1.6 %collective-permute-start.2 = (f32[4,16,128]{2,1,0:T(8,128)S(1)}, f32[4,16,128]{2,1,0:T(8,128)S(1)}, u32[]{:S(2)}, u32[]{:S(2)}) collective-permute-start(f32[4,16,128]{2,1,0:T(8,128)S(1)} %get-tuple-element.30), channel_id=1, source_target_pairs={{0,12},{4,8},{8,4},{12,0},{16,28},{20,24},{24,20},{28,16},{1,13},{... | collective-permute-start | bytes 98312 | tf_op jit(solution)/shard_map/ppermute | solution.py:399
  22.8 0.4 %collective-permute-done.rest_1_ = f32[4,16,128]{2,1,0:T(8,128)S(1)} collective-permute-done((f32[4,16,128]{2,1,0:T(8,128)S(1)}, f32[4,16,128]{2,1,0:T(8,128)S(1)}, u32[]{:S(2)}, u32[]{:S(2)}) %collective-permute-start) | collective-permute-done | bytes 32800 | tf_op jit(solution)/shard_map/ppermute | solution.py:399
  23.2 1.2 %collective-permute-done.1.rest_2_ = f32[4,16,128]{2,1,0:T(8,128)S(1)} collective-permute-done((f32[4,16,128]{2,1,0:T(8,128)S(1)}, f32[4,16,128]{2,1,0:T(8,128)S(1)}, u32[]{:S(2)}, u32[]{:S(2)}) %collective-permute-start.1) | collective-permute-done | bytes 32800 | tf_op jit(solution)/shard_map/ppermute | solution.py:399
  24.4 1.6 %collective-permute-done.2.rest_3_ = f32[4,16,128]{2,1,0:T(8,128)S(1)} collective-permute-done((f32[4,16,128]{2,1,0:T(8,128)S(1)}, f32[4,16,128]{2,1,0:T(8,128)S(1)}, u32[]{:S(2)}, u32[]{:S(2)}) %collective-permute-start.2) | collective-permute-done | bytes 32800 | tf_op jit(solution)/shard_map/ppermute | solution.py:399
  26.0 0.9 %shard_map.66 = f32[32,16,128]{2,1,0:T(8,128)} custom-call(f32[33,16,128]{2,1,0:T(8,128)S(1)} %get-tuple-element.18.power_ref, f32[2,16,128]{2,1,0:T(8,128)S(1)} %get-tuple-element.19.turn_ref, f32[32,16,128]{2,1,0:T(8,128)S(1)} %get-tuple-element.26.near_ref, f32[4,16,128]{2,1,0:T(8,128)S(1)} %get-tuple-element.27.rest_0_, ...), custom_call_target="tpu_custom_call" | custom-call | tf_op jit(solution)/shard_map/pallas_call | solution.py:400
Async XLA Ops:
  19.2 4.0 %collective-permute-start = (f32[4,16,128]{2,1,0:T(8,128)S(1)}, f32[4,16,128]{2,1,0:T(8,128)S(1)}, u32[]{:S(2)}, u32[]{:S(2)}) collective-permute-start(f32[4,16,128]{2,1,0:T(8,128)S(1)} %get-tuple-element.28), channel_id=1, source_target_pairs={{0,4},{4,0},{8,12},{12,8},{16,20},{20,16},{24,28},{28,24},{1,5},{5... | collective-permute-start | bytes 98312 | tf_op jit(solution)/shard_map/ppermute | solution.py:399
  20.5 3.9 %collective-permute-start.1 = (f32[4,16,128]{2,1,0:T(8,128)S(1)}, f32[4,16,128]{2,1,0:T(8,128)S(1)}, u32[]{:S(2)}, u32[]{:S(2)}) collective-permute-start(f32[4,16,128]{2,1,0:T(8,128)S(1)} %get-tuple-element.29), channel_id=1, source_target_pairs={{0,8},{4,12},{8,0},{12,4},{16,24},{20,28},{24,16},{28,20},{1,9},{5... | collective-permute-start | bytes 98312 | tf_op jit(solution)/shard_map/ppermute | solution.py:399
  21.2 4.8 %collective-permute-start.2 = (f32[4,16,128]{2,1,0:T(8,128)S(1)}, f32[4,16,128]{2,1,0:T(8,128)S(1)}, u32[]{:S(2)}, u32[]{:S(2)}) collective-permute-start(f32[4,16,128]{2,1,0:T(8,128)S(1)} %get-tuple-element.30), channel_id=1, source_target_pairs={{0,12},{4,8},{8,4},{12,0},{16,28},{20,24},{24,20},{28,16},{1,13},{... | collective-permute-start | bytes 98312 | tf_op jit(solution)/shard_map/ppermute | solution.py:399

commit v5 on v4

--- a/solution.py
+++ b/solution.py
@@ -151,7 +151,11 @@
             reach = jnp.where(
                 ahead > 1, ZDEV * ahead - (PLANES - 1), jnp.where(ahead < 0, ZDEV * (-ahead - 1), 0)
             )
-            weight_ref[2 * hop + j] = jnp.exp(-kappa * reach.astype(jnp.float32))
+            weight = jnp.exp(-kappa * reach.astype(jnp.float32))
+            for k, joins in enumerate((ahead == 1, ahead > 1, ahead < 0)):
+                weight_ref[6 * hop + 3 * j + k] = jnp.where(joins, weight, 0.0)
+    for j, source in enumerate((slab, far_slab)):
+        weight_ref[6 * half + j] = jnp.full(kappa.shape, jnp.where(source < slabs - 1, 1.0, 0.0))
 
     scale = (sigma * 2.0 / NXD) / kappa
     turn_cos, turn_sin = cos_sin_turns(turns)
@@ -161,7 +165,7 @@
 
 
 def spectrum_kernel(
-    group, slabs, slab_ref, rows_ref, x_ref, y_ref, fine_ref, mask_ref, power_ref, weight_ref, near_ref, *rest
+    group, joined, rows_ref, x_ref, y_ref, fine_ref, mask_ref, power_ref, weight_ref, near_ref, *rest
 ):
     send_refs, (own_ref, far_ref) = rest[:-2], rest[-2:]
     kx_count = x_ref.shape[1]
@@ -248,18 +252,11 @@
 
     lax.fori_loop(0, blocks // group, step, 0)
 
-    half = slabs // 2
-    slab = slab_ref[0]
-    upper = slab >= half
-    first = jnp.where(upper, half, 0)
-    member = slab - first
-    far_slab = jnp.where(upper, slab - half, slab + half)
     decay = power_ref[1]
     width = 2 * ky_count
 
     def plane_of(acc_ref, z):
-        start = z * kx_count
-        both = acc_ref[pl.ds(start if isinstance(z, int) else pl.multiple_of(start, kx_count), kx_count), :]
+        both = acc_ref[z * kx_count : (z + 1) * kx_count, :]
         plane = both[:, :width] + both[:, width:]
         if acc_ref is own_ref:
             first = PLANES * kx_count + FINE * z
@@ -267,54 +264,47 @@
                 plane = plane + mask_ref[j] * acc_ref[first + j : first + j + 1, :width]
         return plane
 
-    def spills_of(acc_ref, index):
-        inside = jnp.where(index < slabs - 1, 1.0, 0.0)
-        return [plane_of(acc_ref, ZDEV + j) * inside for j in range(SPILL)]
-
-    spilled = spills_of(own_ref, slab)
-    down = spilled[0] + decay * (spilled[1] + decay * spilled[2])
-    for z in range(ZDEV - 1, -1, -1):
-        down = decay * down
-        near_ref[z] = down
-        down = plane_of(own_ref, z) + down
-    up = jnp.zeros_like(decay)
-    for z in range(ZDEV):
-        up = plane_of(own_ref, z) + decay * up
-        near_ref[z] += up
-    up_near = spilled[0] + decay * up
-    up_far = spilled[2] + decay * (spilled[1] + decay * up_near)
-
-    far_spilled = spills_of(far_ref, far_slab)
-    moment = jnp.where(
-        upper, jnp.zeros_like(decay), far_spilled[0] + decay * (far_spilled[1] + decay * far_spilled[2])
-    )
-    for j in range(ZDEV):
-        moment = plane_of(far_ref, jnp.where(upper, j, ZDEV - 1 - j)) + decay * moment
-    far_near = far_spilled[0] + decay * moment
-    far_far = far_spilled[2] + decay * (far_spilled[1] + decay * far_near)
+    parts = []
+    for j, acc_ref in enumerate((own_ref, far_ref)):
+        inside = weight_ref[6 * len(send_refs) + j]
+        spilled = [plane_of(acc_ref, ZDEV + k) * inside for k in range(SPILL)]
+        down = spilled[0] + decay * (spilled[1] + decay * spilled[2])
+        for z in range(ZDEV - 1, -1, -1):
+            down = decay * down
+            if j == 0:
+                near_ref[z] = down
+            down = plane_of(acc_ref, z) + down
+        up = jnp.zeros_like(decay)
+        for z in range(ZDEV):
+            up = plane_of(acc_ref, z) + decay * up
+            if j == 0:
+                near_ref[z] += up
+        up_near = spilled[0] + decay * up
+        up_far = spilled[2] + decay * (spilled[1] + decay * up_near)
+        parts.append((spilled, up_near, up_far, down))
 
     for hop, send_ref in enumerate(send_refs):
-        target = first + partner(member, hop, half)
-        zero = jnp.zeros_like(decay)
-        ahead = target - slab
-        own_weight = weight_ref[2 * hop]
-        own_low = jnp.where(ahead > 0, own_weight * jnp.where(ahead == 1, up_near, up_far), zero)
-        own_high = jnp.where(ahead < 0, own_weight * down, zero)
-        far_ahead = target - far_slab
-        far_weight = weight_ref[2 * hop + 1]
-        far_low = jnp.where(upper, far_weight * jnp.where(far_ahead == 1, far_near, far_far), zero)
-        far_high = jnp.where(upper, zero, far_weight * moment)
-        send_ref[0] = own_low + far_low
-        send_ref[1] = own_high + far_high
-        for j in (1, 2):
-            send_ref[1 + j] = jnp.where(
-                ahead == 1, spilled[j], jnp.where(far_ahead == 1, far_spilled[j], zero)
-            )
+        low = high = first = second = 0.0
+        for j, (spilled, up_near, up_far, down) in enumerate(parts):
+            near_above, above, below = (weight_ref[6 * hop + 3 * j + k] for k in range(3))
+            low = low + above * up_far
+            high = high + below * down
+            if joined[hop]:
+                low = low + near_above * up_near
+                first = first + near_above * spilled[1]
+                second = second + near_above * spilled[2]
+        send_ref[0] = low
+        send_ref[1] = high
+        if joined[hop]:
+            send_ref[2] = first
+            send_ref[3] = second
 
 
 def far_kernel(power_ref, turn_ref, near_ref, *rest):
     received_refs, out_ref = rest[:-1], rest[-1]
-    low, high, first, second = (sum(ref[part] for ref in received_refs) for part in range(4))
+    low, high, first, second = (
+        sum(ref[part] for ref in received_refs if part < ref.shape[0]) for part in range(4)
+    )
     decay = power_ref[1]
     turn_cos, turn_sin = turn_ref[0], turn_ref[1]
     low_at = [
@@ -353,7 +343,7 @@
         shaped(6, 8, 128),
         shaped(FINE, kx_local, width),
         shaped(ZDEV + 1, kx_local, width),
-        shaped(2 * half, kx_local, width),
+        shaped(6 * half + 2, kx_local, width),
         shaped(2, kx_local, width),
     )
     inputs = (
@@ -378,20 +368,22 @@
     blocks = arrived.shape[0] // 16
     group = math.gcd(blocks, 16)
     planes = shaped(ZDEV, kx_local, width)
-    message = shaped(4, kx_local, width)
+    joined = [
+        any(partner(m, hop, half) == (m + 1) % half for m in range(half)) for hop in range(half)
+    ]
     coarse_rows = PLANES * kx_local
     fine_rows = FINE * 8 * pl.cdiv(PLANES, 8)
     near, *messages = pl.pallas_call(
-        functools.partial(spectrum_kernel, group, slabs),
-        out_shape=(planes,) + (message,) * half,
-        in_specs=[smem] + [vmem] * (1 + len(tables)),
+        functools.partial(spectrum_kernel, group, joined),
+        out_shape=(planes,) + tuple(shaped(4 if joins else 2, kx_local, width) for joins in joined),
+        in_specs=[vmem] * (1 + len(tables)),
         out_specs=(vmem,) * (1 + half),
         scratch_shapes=[
             pltpu.VMEM((coarse_rows + fine_rows, 2 * width), jnp.float32),
             pltpu.VMEM((coarse_rows, 2 * width), jnp.float32),
         ],
         compiler_params=pltpu.CompilerParams(vmem_limit_bytes=40 * 1024 * 1024),
-    )(slab, arrived, *tables)
+    )(arrived, *tables)
 
     received = messages[:1]
     for hop in range(1, half):

time: 27 us -> 26.4 us (0.978)
  waiting for transfers between devices: 3.22 us -> 2.73 us
    ppermute x3, waiting for transfers between devices: 3.22 us -> 2.73 us  [shards(): received.append(lax.ppermute(messages[hop], 'gz', pairs))]
  transfers between devices with their start and end apart: 3 -> 3, of which waited for: 3 -> 1; matrix products, arithmetic and copies ran while one was open for 0% -> 0% of each run, Pallas kernels for 0% -> 0%
where the time goes in v5:
time: 26.4 us; the launch traced here: 26.2 us
  blocking collectives  14.8 us (56%)
  Pallas kernels  5.08 us (19%)
  starting transfers between devices  3.55 us (13%)
  waiting for transfers between devices  2.73 us (10%)
    all_to_all x1, blocking collectives, shards(): lax.all_to_all(sent, ('gx', 'gz'), split_axis=0, concat_axis=0, tiled=True)  14.8 us
    ppermute x3, starting transfers between devices, shards(): received.append(lax.ppermute(messages[hop], 'gz', pairs))  3.55 us
    pallas_call x1, Pallas kernels, shards(): pl.pallas_call(functools.partial(spectrum_kernel, group, joined), out_sha...  3.19 us
    ppermute x3, waiting for transfers between devices, shards(): received.append(lax.ppermute(messages[hop], 'gz', pairs))  2.73 us
    pallas_call x1, Pallas kernels, shards(): pl.pallas_call(functools.partial(prepare_kernel, slabs), out_shape=prepar...  1.04 us
    pallas_call x1, Pallas kernels, shards(): pl.pallas_call(far_kernel, out_shape=planes, in_specs=[vmem] * (3 + half)...  0.86 us
  transfers between devices with their start and end apart: 3, of which 1 were waited for; matrix products, arithmetic and copies ran while one was open for 0% of the time, Pallas kernels for 0%

profile of v5, /device:TPU:0, one launch (start us, length us, event | category | flops | bytes accessed | tf_op | source)
XLA Modules:
  0.0 26.2 jit_solution(3910669420887273839)
XLA Ops:
  0.0 1.0 %shard_map.64 = (f32[256,128]{1,0:T(8,128)S(1)}, f32[6,16,128]{2,1,0:T(8,128)S(1)}, f32[6,64,128]{2,1,0:T(8,128)S(1)}, f32[6,8,128]{2,1,0:T(8,128)S(1)}, f32[2,1...) custom-call(s32[1]{0:T(128)} %bitcast.slab_ref, ...), custom_call_target="tpu_custom_call" | custom-call | tf_op jit(solution)/shard_map/pallas_call | solution.py:356
  1.0 14.8 %all_to_all.5 = f32[32,8,128]{2,1,0:T(8,128)S(1)} all-to-all(f32[32,8,128]{2,1,0:T(8,128)S(1)} %bitcast.14), channel_id=1, replica_groups=mesh['gz'=8,'gx'=4] {'gx','gz'}, dimensions={0} | all-to-all | bytes 262144 | tf_op jit(solution)/shard_map/all_to_all | solution.py:365
  15.9 3.2 %shard_map.65 = (f32[32,16,128]{2,1,0:T(8,128)S(1)}, f32[2,16,128]{2,1,0:T(8,128)S(1)}, f32[4,16,128]{2,1,0:T(8,128)S(1)}, f32[2,16,128]{2,1,0:T(8,128)S(1)}, f32[4,16,128]{2,1,0:T(8,128)S(1)}) custom-call(f32[256,128]{1,0:T(8,128)S(1)} %bitcast.13, f32[6,16,128]{2,1,0:T(8,128)S(1)} %get-tuple-element.21.x_ref, f32[6,64,128]{2,1,0:T(8,128)S(1)} %get-tuple-element.22.y_ref, ...), custom_call_target="tpu_custom_call" | custom-call | tf_op jit(solution)/shard_map/pallas_call | solution.py:376
  19.1 1.3 %collective-permute-start = (f32[4,16,128]{2,1,0:T(8,128)S(1)}, f32[4,16,128]{2,1,0:T(8,128)S(1)}, u32[]{:S(2)}, u32[]{:S(2)}) collective-permute-start(f32[4,16,128]{2,1,0:T(8,128)S(1)} %get-tuple-element.28), channel_id=1, source_target_pairs={{0,4},{4,0},{8,12},{12,8},{16,20},{20,16},{24,28},{28,24},{1,5},{5... | collective-permute-start | bytes 98312 | tf_op jit(solution)/shard_map/ppermute | solution.py:391
  20.4 1.2 %collective-permute-start.2 = (f32[4,16,128]{2,1,0:T(8,128)S(1)}, f32[4,16,128]{2,1,0:T(8,128)S(1)}, u32[]{:S(2)}, u32[]{:S(2)}) collective-permute-start(f32[4,16,128]{2,1,0:T(8,128)S(1)} %get-tuple-element.30), channel_id=1, source_target_pairs={{0,12},{4,8},{8,4},{12,0},{16,28},{20,24},{24,20},{28,16},{1,13},{... | collective-permute-start | bytes 98312 | tf_op jit(solution)/shard_map/ppermute | solution.py:391
  21.6 1.0 %collective-permute-start.1 = (f32[2,16,128]{2,1,0:T(8,128)S(1)}, f32[2,16,128]{2,1,0:T(8,128)S(1)}, u32[]{:S(2)}, u32[]{:S(2)}) collective-permute-start(f32[2,16,128]{2,1,0:T(8,128)S(1)} %get-tuple-element.29), channel_id=1, source_target_pairs={{0,8},{4,12},{8,0},{12,4},{16,24},{20,28},{24,16},{28,20},{1,9},{5... | collective-permute-start | bytes 49160 | tf_op jit(solution)/shard_map/ppermute | solution.py:391
  22.6 2.7 %collective-permute-done.1.rest_2_ = f32[2,16,128]{2,1,0:T(8,128)S(1)} collective-permute-done((f32[2,16,128]{2,1,0:T(8,128)S(1)}, f32[2,16,128]{2,1,0:T(8,128)S(1)}, u32[]{:S(2)}, u32[]{:S(2)}) %collective-permute-start.1) | collective-permute-done | bytes 16416 | tf_op jit(solution)/shard_map/ppermute | solution.py:391
  25.4 0.0 collective-permute-done.rest_1_
  25.4 0.0 collective-permute-done.2.rest_3_
  25.4 0.9 %shard_map.66 = f32[32,16,128]{2,1,0:T(8,128)} custom-call(f32[33,16,128]{2,1,0:T(8,128)S(1)} %get-tuple-element.18.power_ref, f32[2,16,128]{2,1,0:T(8,128)S(1)} %get-tuple-element.19.turn_ref, f32[32,16,128]{2,1,0:T(8,128)S(1)} %get-tuple-element.26.near_ref, f32[2,16,128]{2,1,0:T(8,128)S(1)} %get-tuple-element.27.rest_0_, ...), custom_call_target="tpu_custom_call" | custom-call | tf_op jit(solution)/shard_map/pallas_call | solution.py:392
Async XLA Ops:
  19.1 6.3 %collective-permute-start = (f32[4,16,128]{2,1,0:T(8,128)S(1)}, f32[4,16,128]{2,1,0:T(8,128)S(1)}, u32[]{:S(2)}, u32[]{:S(2)}) collective-permute-start(f32[4,16,128]{2,1,0:T(8,128)S(1)} %get-tuple-element.28), channel_id=1, source_target_pairs={{0,4},{4,0},{8,12},{12,8},{16,20},{20,16},{24,28},{28,24},{1,5},{5... | collective-permute-start | bytes 98312 | tf_op jit(solution)/shard_map/ppermute | solution.py:391
  20.4 5.0 %collective-permute-start.2 = (f32[4,16,128]{2,1,0:T(8,128)S(1)}, f32[4,16,128]{2,1,0:T(8,128)S(1)}, u32[]{:S(2)}, u32[]{:S(2)}) collective-permute-start(f32[4,16,128]{2,1,0:T(8,128)S(1)} %get-tuple-element.30), channel_id=1, source_target_pairs={{0,12},{4,8},{8,4},{12,0},{16,28},{20,24},{24,20},{28,16},{1,13},{... | collective-permute-start | bytes 98312 | tf_op jit(solution)/shard_map/ppermute | solution.py:391
  21.6 3.7 %collective-permute-start.1 = (f32[2,16,128]{2,1,0:T(8,128)S(1)}, f32[2,16,128]{2,1,0:T(8,128)S(1)}, u32[]{:S(2)}, u32[]{:S(2)}) collective-permute-start(f32[2,16,128]{2,1,0:T(8,128)S(1)} %get-tuple-element.29), channel_id=1, source_target_pairs={{0,8},{4,12},{8,0},{12,4},{16,24},{20,28},{24,16},{28,20},{1,9},{5... | collective-permute-start | bytes 49160 | tf_op jit(solution)/shard_map/ppermute | solution.py:391

commit v6 on v5

--- a/solution.py
+++ b/solution.py
@@ -48,14 +48,21 @@
     return cos_sin_turns(0.5 * freq) + cos_sin_turns(1.5 * freq)
 
 
-def transform(table_ref, column, side, pairs):
+def lookup(table_ref, column, side):
     column = jnp.broadcast_to(column, table_ref.shape[1:])
     c = jnp.take_along_axis(table_ref[0], column, axis=1)
-    s = jnp.take_along_axis(table_ref[1], column, axis=1) * side
+    return c, jnp.take_along_axis(table_ref[1], column, axis=1) * side
+
+
+def turned(c, s, table_ref, pairs):
     even1, odd1, even3, odd3 = pairs
     re = even1 * table_ref[2] + even3 * table_ref[4]
     im = odd1 * table_ref[3] + odd3 * table_ref[5]
     return c * re - s * im, s * re + c * im
+
+
+def transform(table_ref, column, side, pairs):
+    return turned(*lookup(table_ref, column, side), table_ref, pairs)
 
 
 def node_pairs(weights):
@@ -198,19 +205,31 @@
                 jnp.concatenate([(here * cx).astype(jnp.bfloat16), (here * sx).astype(jnp.bfloat16)], axis=1)
             )
         if row == 0:
-            fine_c, fine_s = transform(fine_ref, column_x, side_x, wx)
+            wz_rows = jnp.concatenate([w for w in wz for _ in range(FINE)], axis=0)
+            deposited = [
+                (wz_rows * w[row + 1 : row + 2]).astype(jnp.bfloat16).astype(jnp.float32) for w in weights
+            ]
+            fine_c, fine_s = lookup(fine_ref, column_x, side_x)
+            exact = turned(fine_c, fine_s, fine_ref, node_pairs(deposited))
+            plain = turned(fine_c, fine_s, fine_ref, wx)
+            lacks = [
+                e - (wz_rows * p).astype(jnp.bfloat16).astype(jnp.float32) for e, p in zip(exact, plain)
+            ]
+            shift = base_z.astype(jnp.int32) * FINE
             for z in range(0, spread.shape[0], 8):
-                here = [
-                    jnp.take_along_axis(spread[z : z + 8], (fine_row >> 1) + half, axis=0)
-                    for half in range(0, 8, 8 // FINE)
-                ]
+                tiles = []
+                for first in (z, z + 4):
+                    if first >= PLANES:
+                        tiles.append([jnp.zeros((8, 128), jnp.float32)] * 2)
+                        continue
+                    source = fine_row + FINE * first - shift
+                    held = (source & 7) == source
+                    tiles.append(
+                        [jnp.where(held, jnp.take_along_axis(r, source & 7, axis=0), 0.0) for r in lacks]
+                    )
                 lhs.append(
                     jnp.concatenate(
-                        [
-                            two_parts(jnp.concatenate([h * part for h in here], axis=0))[1]
-                            for part in (fine_c, fine_s)
-                        ],
-                        axis=1,
+                        [jnp.concatenate(pair, axis=0).astype(jnp.bfloat16) for pair in zip(*tiles)], axis=1
                     )
                 )
         cy_high, cy_low = two_parts(cy)
@@ -223,9 +242,9 @@
 
     def one_block(block):
         rows = rows_ref[pl.ds(pl.multiple_of(block * 16, 16), 16), :]
-        turned = pltpu.roll(rows, 64, axis=1)
-        frac = jnp.where(low_lanes, rows[0:8], turned[8:16])
-        cell = jnp.where(low_lanes, turned[0:8], rows[8:16])
+        rolled = pltpu.roll(rows, 64, axis=1)
+        frac = jnp.where(low_lanes, rows[0:8], rolled[8:16])
+        cell = jnp.where(low_lanes, rolled[0:8], rows[8:16])
         weights = node_weights(frac)
         column = jnp.abs(cell - MIDDLE).astype(jnp.int32)
         side = jnp.where(cell < MIDDLE, -1.0, 1.0)

time: 26.4 us -> 26.6 us (level)
  no operation moved by 1% of the time
where the time goes in v6:
time: 26.6 us; the launch traced here: 26.4 us
  blocking collectives  14.8 us (56%)
  Pallas kernels  5.24 us (20%)
  starting transfers between devices  3.55 us (13%)
  waiting for transfers between devices  2.73 us (10%)
    all_to_all x1, blocking collectives, shards(): lax.all_to_all(sent, ('gx', 'gz'), split_axis=0, concat_axis=0, tiled=True)  14.8 us
    ppermute x3, starting transfers between devices, shards(): received.append(lax.ppermute(messages[hop], 'gz', pairs))  3.55 us
    pallas_call x1, Pallas kernels, shards(): pl.pallas_call(functools.partial(spectrum_kernel, group, joined), out_sha...  3.35 us
    ppermute x3, waiting for transfers between devices, shards(): received.append(lax.ppermute(messages[hop], 'gz', pairs))  2.73 us
    pallas_call x1, Pallas kernels, shards(): pl.pallas_call(functools.partial(prepare_kernel, slabs), out_shape=prepar...  1.04 us
    pallas_call x1, Pallas kernels, shards(): pl.pallas_call(far_kernel, out_shape=planes, in_specs=[vmem] * (3 + half)...  0.86 us
  transfers between devices with their start and end apart: 3, of which 1 were waited for; matrix products, arithmetic and copies ran while one was open for 0% of the time, Pallas kernels for 0%

profile of v6, /device:TPU:0, one launch (start us, length us, event | category | flops | bytes accessed | tf_op | source)
XLA Modules:
  0.0 26.4 jit_solution(18157159613098634876)
XLA Ops:
  0.0 1.0 %shard_map.64 = (f32[256,128]{1,0:T(8,128)S(1)}, f32[6,16,128]{2,1,0:T(8,128)S(1)}, f32[6,64,128]{2,1,0:T(8,128)S(1)}, f32[6,8,128]{2,1,0:T(8,128)S(1)}, f32[2,1...) custom-call(s32[1]{0:T(128)} %bitcast.slab_ref, ...), custom_call_target="tpu_custom_call" | custom-call | tf_op jit(solution)/shard_map/pallas_call | solution.py:375
  1.0 14.8 %all_to_all.5 = f32[32,8,128]{2,1,0:T(8,128)S(1)} all-to-all(f32[32,8,128]{2,1,0:T(8,128)S(1)} %bitcast.14), channel_id=1, replica_groups=mesh['gz'=8,'gx'=4] {'gx','gz'}, dimensions={0} | all-to-all | bytes 262144 | tf_op jit(solution)/shard_map/all_to_all | solution.py:384
  15.9 3.3 %shard_map.65 = (f32[32,16,128]{2,1,0:T(8,128)S(1)}, f32[2,16,128]{2,1,0:T(8,128)S(1)}, f32[4,16,128]{2,1,0:T(8,128)S(1)}, f32[2,16,128]{2,1,0:T(8,128)S(1)}, f32[4,16,128]{2,1,0:T(8,128)S(1)}) custom-call(f32[256,128]{1,0:T(8,128)S(1)} %bitcast.13, f32[6,16,128]{2,1,0:T(8,128)S(1)} %get-tuple-element.21.x_ref, f32[6,64,128]{2,1,0:T(8,128)S(1)} %get-tuple-element.22.y_ref, ...), custom_call_target="tpu_custom_call" | custom-call | tf_op jit(solution)/shard_map/pallas_call | solution.py:395
  19.2 1.3 %collective-permute-start = (f32[4,16,128]{2,1,0:T(8,128)S(1)}, f32[4,16,128]{2,1,0:T(8,128)S(1)}, u32[]{:S(2)}, u32[]{:S(2)}) collective-permute-start(f32[4,16,128]{2,1,0:T(8,128)S(1)} %get-tuple-element.28), channel_id=1, source_target_pairs={{0,4},{4,0},{8,12},{12,8},{16,20},{20,16},{24,28},{28,24},{1,5},{5... | collective-permute-start | bytes 98312 | tf_op jit(solution)/shard_map/ppermute | solution.py:410
  20.5 1.2 %collective-permute-start.2 = (f32[4,16,128]{2,1,0:T(8,128)S(1)}, f32[4,16,128]{2,1,0:T(8,128)S(1)}, u32[]{:S(2)}, u32[]{:S(2)}) collective-permute-start(f32[4,16,128]{2,1,0:T(8,128)S(1)} %get-tuple-element.30), channel_id=1, source_target_pairs={{0,12},{4,8},{8,4},{12,0},{16,28},{20,24},{24,20},{28,16},{1,13},{... | collective-permute-start | bytes 98312 | tf_op jit(solution)/shard_map/ppermute | solution.py:410
  21.8 1.0 %collective-permute-start.1 = (f32[2,16,128]{2,1,0:T(8,128)S(1)}, f32[2,16,128]{2,1,0:T(8,128)S(1)}, u32[]{:S(2)}, u32[]{:S(2)}) collective-permute-start(f32[2,16,128]{2,1,0:T(8,128)S(1)} %get-tuple-element.29), channel_id=1, source_target_pairs={{0,8},{4,12},{8,0},{12,4},{16,24},{20,28},{24,16},{28,20},{1,9},{5... | collective-permute-start | bytes 49160 | tf_op jit(solution)/shard_map/ppermute | solution.py:410
  22.8 2.7 %collective-permute-done.1.rest_2_ = f32[2,16,128]{2,1,0:T(8,128)S(1)} collective-permute-done((f32[2,16,128]{2,1,0:T(8,128)S(1)}, f32[2,16,128]{2,1,0:T(8,128)S(1)}, u32[]{:S(2)}, u32[]{:S(2)}) %collective-permute-start.1) | collective-permute-done | bytes 16416 | tf_op jit(solution)/shard_map/ppermute | solution.py:410
  25.5 0.0 collective-permute-done.rest_1_
  25.5 0.0 collective-permute-done.2.rest_3_
  25.5 0.9 %shard_map.66 = f32[32,16,128]{2,1,0:T(8,128)} custom-call(f32[33,16,128]{2,1,0:T(8,128)S(1)} %get-tuple-element.18.power_ref, f32[2,16,128]{2,1,0:T(8,128)S(1)} %get-tuple-element.19.turn_ref, f32[32,16,128]{2,1,0:T(8,128)S(1)} %get-tuple-element.26.near_ref, f32[2,16,128]{2,1,0:T(8,128)S(1)} %get-tuple-element.27.rest_0_, ...), custom_call_target="tpu_custom_call" | custom-call | tf_op jit(solution)/shard_map/pallas_call | solution.py:411
Async XLA Ops:
  19.2 6.3 %collective-permute-start = (f32[4,16,128]{2,1,0:T(8,128)S(1)}, f32[4,16,128]{2,1,0:T(8,128)S(1)}, u32[]{:S(2)}, u32[]{:S(2)}) collective-permute-start(f32[4,16,128]{2,1,0:T(8,128)S(1)} %get-tuple-element.28), channel_id=1, source_target_pairs={{0,4},{4,0},{8,12},{12,8},{16,20},{20,16},{24,28},{28,24},{1,5},{5... | collective-permute-start | bytes 98312 | tf_op jit(solution)/shard_map/ppermute | solution.py:410
  20.5 5.0 %collective-permute-start.2 = (f32[4,16,128]{2,1,0:T(8,128)S(1)}, f32[4,16,128]{2,1,0:T(8,128)S(1)}, u32[]{:S(2)}, u32[]{:S(2)}) collective-permute-start(f32[4,16,128]{2,1,0:T(8,128)S(1)} %get-tuple-element.30), channel_id=1, source_target_pairs={{0,12},{4,8},{8,4},{12,0},{16,28},{20,24},{24,20},{28,16},{1,13},{... | collective-permute-start | bytes 98312 | tf_op jit(solution)/shard_map/ppermute | solution.py:410
  21.8 3.7 %collective-permute-start.1 = (f32[2,16,128]{2,1,0:T(8,128)S(1)}, f32[2,16,128]{2,1,0:T(8,128)S(1)}, u32[]{:S(2)}, u32[]{:S(2)}) collective-permute-start(f32[2,16,128]{2,1,0:T(8,128)S(1)} %get-tuple-element.29), channel_id=1, source_target_pairs={{0,8},{4,12},{8,0},{12,4},{16,24},{20,28},{24,16},{28,20},{1,9},{5... | collective-permute-start | bytes 49160 | tf_op jit(solution)/shard_map/ppermute | solution.py:410

commit v7 on v6

--- a/solution.py
+++ b/solution.py
@@ -234,10 +234,10 @@
                 )
         cy_high, cy_low = two_parts(cy)
         sy_high, sy_low = two_parts(-sy)
-        rhs = [
-            jnp.concatenate(pair, axis=1)
-            for pair in ((cy_high, sy_high), (sy_high, -cy_high), (cy_low, sy_low), (sy_low, -cy_low))
-        ]
+        pairs = [(cy_high, sy_high), (sy_high, -cy_high)]
+        if row == 0:
+            pairs += [(cy_low, sy_low), (sy_low, -cy_low)]
+        rhs = [jnp.concatenate(pair, axis=1) for pair in pairs]
         return jnp.concatenate(lhs, axis=0), jnp.concatenate(rhs, axis=0)
 
     def one_block(block):
@@ -276,7 +276,7 @@
 
     def plane_of(acc_ref, z):
         both = acc_ref[z * kx_count : (z + 1) * kx_count, :]
-        plane = both[:, :width] + both[:, width:]
+        plane = both[:, :width] + both[:, width:] if acc_ref is own_ref else both
         if acc_ref is own_ref:
             first = PLANES * kx_count + FINE * z
             for j in range(FINE):
@@ -399,7 +399,7 @@
         out_specs=(vmem,) * (1 + half),
         scratch_shapes=[
             pltpu.VMEM((coarse_rows + fine_rows, 2 * width), jnp.float32),
-            pltpu.VMEM((coarse_rows, 2 * width), jnp.float32),
+            pltpu.VMEM((coarse_rows, width), jnp.float32),
         ],
         compiler_params=pltpu.CompilerParams(vmem_limit_bytes=40 * 1024 * 1024),
     )(arrived, *tables)

time: 26.6 us -> 26.4 us (level)
  no operation moved by 1% of the time
where the time goes in v7:
time: 26.4 us; the launch traced here: 26.3 us
  blocking collectives  14.8 us (56%)
  Pallas kernels  5.12 us (19%)
  starting transfers between devices  3.55 us (13%)
  waiting for transfers between devices  2.74 us (10%)
    all_to_all x1, blocking collectives, shards(): lax.all_to_all(sent, ('gx', 'gz'), split_axis=0, concat_axis=0, tiled=True)  14.8 us
    ppermute x3, starting transfers between devices, shards(): received.append(lax.ppermute(messages[hop], 'gz', pairs))  3.55 us
    pallas_call x1, Pallas kernels, shards(): pl.pallas_call(functools.partial(spectrum_kernel, group, joined), out_sha...  3.22 us
    ppermute x3, waiting for transfers between devices, shards(): received.append(lax.ppermute(messages[hop], 'gz', pairs))  2.74 us
    pallas_call x1, Pallas kernels, shards(): pl.pallas_call(functools.partial(prepare_kernel, slabs), out_shape=prepar...  1.04 us
    pallas_call x1, Pallas kernels, shards(): pl.pallas_call(far_kernel, out_shape=planes, in_specs=[vmem] * (3 + half)...  0.86 us
  transfers between devices with their start and end apart: 3, of which 1 were waited for; matrix products, arithmetic and copies ran while one was open for 0% of the time, Pallas kernels for 0%

profile of v7, /device:TPU:0, one launch (start us, length us, event | category | flops | bytes accessed | tf_op | source)
XLA Modules:
  0.0 26.3 jit_solution(17540348049035135346)
XLA Ops:
  0.0 1.0 %shard_map.64 = (f32[256,128]{1,0:T(8,128)S(1)}, f32[6,16,128]{2,1,0:T(8,128)S(1)}, f32[6,64,128]{2,1,0:T(8,128)S(1)}, f32[6,8,128]{2,1,0:T(8,128)S(1)}, f32[2,1...) custom-call(s32[1]{0:T(128)} %bitcast.slab_ref, ...), custom_call_target="tpu_custom_call" | custom-call | tf_op jit(solution)/shard_map/pallas_call | solution.py:375
  1.0 14.8 %all_to_all.5 = f32[32,8,128]{2,1,0:T(8,128)S(1)} all-to-all(f32[32,8,128]{2,1,0:T(8,128)S(1)} %bitcast.14), channel_id=1, replica_groups=mesh['gz'=8,'gx'=4] {'gx','gz'}, dimensions={0} | all-to-all | bytes 262144 | tf_op jit(solution)/shard_map/all_to_all | solution.py:384
  15.9 3.2 %shard_map.65 = (f32[32,16,128]{2,1,0:T(8,128)S(1)}, f32[2,16,128]{2,1,0:T(8,128)S(1)}, f32[4,16,128]{2,1,0:T(8,128)S(1)}, f32[2,16,128]{2,1,0:T(8,128)S(1)}, f32[4,16,128]{2,1,0:T(8,128)S(1)}) custom-call(f32[256,128]{1,0:T(8,128)S(1)} %bitcast.13, f32[6,16,128]{2,1,0:T(8,128)S(1)} %get-tuple-element.21.x_ref, f32[6,64,128]{2,1,0:T(8,128)S(1)} %get-tuple-element.22.y_ref, ...), custom_call_target="tpu_custom_call" | custom-call | tf_op jit(solution)/shard_map/pallas_call | solution.py:395
  19.1 1.3 %collective-permute-start = (f32[4,16,128]{2,1,0:T(8,128)S(1)}, f32[4,16,128]{2,1,0:T(8,128)S(1)}, u32[]{:S(2)}, u32[]{:S(2)}) collective-permute-start(f32[4,16,128]{2,1,0:T(8,128)S(1)} %get-tuple-element.28), channel_id=1, source_target_pairs={{0,4},{4,0},{8,12},{12,8},{16,20},{20,16},{24,28},{28,24},{1,5},{5... | collective-permute-start | bytes 98312 | tf_op jit(solution)/shard_map/ppermute | solution.py:410
  20.4 1.2 %collective-permute-start.2 = (f32[4,16,128]{2,1,0:T(8,128)S(1)}, f32[4,16,128]{2,1,0:T(8,128)S(1)}, u32[]{:S(2)}, u32[]{:S(2)}) collective-permute-start(f32[4,16,128]{2,1,0:T(8,128)S(1)} %get-tuple-element.30), channel_id=1, source_target_pairs={{0,12},{4,8},{8,4},{12,0},{16,28},{20,24},{24,20},{28,16},{1,13},{... | collective-permute-start | bytes 98312 | tf_op jit(solution)/shard_map/ppermute | solution.py:410
  21.7 1.0 %collective-permute-start.1 = (f32[2,16,128]{2,1,0:T(8,128)S(1)}, f32[2,16,128]{2,1,0:T(8,128)S(1)}, u32[]{:S(2)}, u32[]{:S(2)}) collective-permute-start(f32[2,16,128]{2,1,0:T(8,128)S(1)} %get-tuple-element.29), channel_id=1, source_target_pairs={{0,8},{4,12},{8,0},{12,4},{16,24},{20,28},{24,16},{28,20},{1,9},{5... | collective-permute-start | bytes 49160 | tf_op jit(solution)/shard_map/ppermute | solution.py:410
  22.7 2.7 %collective-permute-done.1.rest_2_ = f32[2,16,128]{2,1,0:T(8,128)S(1)} collective-permute-done((f32[2,16,128]{2,1,0:T(8,128)S(1)}, f32[2,16,128]{2,1,0:T(8,128)S(1)}, u32[]{:S(2)}, u32[]{:S(2)}) %collective-permute-start.1) | collective-permute-done | bytes 16416 | tf_op jit(solution)/shard_map/ppermute | solution.py:410
  25.4 0.0 collective-permute-done.rest_1_
  25.4 0.0 collective-permute-done.2.rest_3_
  25.4 0.9 %shard_map.66 = f32[32,16,128]{2,1,0:T(8,128)} custom-call(f32[33,16,128]{2,1,0:T(8,128)S(1)} %get-tuple-element.18.power_ref, f32[2,16,128]{2,1,0:T(8,128)S(1)} %get-tuple-element.19.turn_ref, f32[32,16,128]{2,1,0:T(8,128)S(1)} %get-tuple-element.26.near_ref, f32[2,16,128]{2,1,0:T(8,128)S(1)} %get-tuple-element.27.rest_0_, ...), custom_call_target="tpu_custom_call" | custom-call | tf_op jit(solution)/shard_map/pallas_call | solution.py:411
Async XLA Ops:
  19.1 6.3 %collective-permute-start = (f32[4,16,128]{2,1,0:T(8,128)S(1)}, f32[4,16,128]{2,1,0:T(8,128)S(1)}, u32[]{:S(2)}, u32[]{:S(2)}) collective-permute-start(f32[4,16,128]{2,1,0:T(8,128)S(1)} %get-tuple-element.28), channel_id=1, source_target_pairs={{0,4},{4,0},{8,12},{12,8},{16,20},{20,16},{24,28},{28,24},{1,5},{5... | collective-permute-start | bytes 98312 | tf_op jit(solution)/shard_map/ppermute | solution.py:410
  20.4 5.0 %collective-permute-start.2 = (f32[4,16,128]{2,1,0:T(8,128)S(1)}, f32[4,16,128]{2,1,0:T(8,128)S(1)}, u32[]{:S(2)}, u32[]{:S(2)}) collective-permute-start(f32[4,16,128]{2,1,0:T(8,128)S(1)} %get-tuple-element.30), channel_id=1, source_target_pairs={{0,12},{4,8},{8,4},{12,0},{16,28},{20,24},{24,20},{28,16},{1,13},{... | collective-permute-start | bytes 98312 | tf_op jit(solution)/shard_map/ppermute | solution.py:410
  21.7 3.7 %collective-permute-start.1 = (f32[2,16,128]{2,1,0:T(8,128)S(1)}, f32[2,16,128]{2,1,0:T(8,128)S(1)}, u32[]{:S(2)}, u32[]{:S(2)}) collective-permute-start(f32[2,16,128]{2,1,0:T(8,128)S(1)} %get-tuple-element.29), channel_id=1, source_target_pairs={{0,8},{4,12},{8,0},{12,4},{16,24},{20,28},{24,16},{28,20},{1,9},{5... | collective-permute-start | bytes 49160 | tf_op jit(solution)/shard_map/ppermute | solution.py:410
